TPU v7x, 32 devices: a whole 2x2x4 slice. The times are simulated.
32 devices in a mesh: grp: 2 (over x), ang: 16 (over z, y, core).
Axes of the slice: x: 2, y: 2, z: 4, core: 2. Of those that a mesh axis runs over, the one named last changes fastest.
Arguments:
- children: bfloat16 [2, 32, 8, 2, 1, 2048], P(None, ('grp', 'ang')), may hold values from -6 to 6
- present: int32 [32, 8], P(('grp', 'ang')), may hold values 0 or 1
- interp: float32 [8, 8192], replicated, may hold values from -2 to 2
- phase: float32 [8, 8192], replicated, may hold values from -3.140625 to 3.140625
- trans: float32 [2, 316, 8192], P(None, None, 'ang'), may hold values from -0.6 to 0.6
- sources: int32 [32, 8], P('grp'), may hold values from 0 to 31
- trans_ids: int32 [32, 8], P('grp'), may hold values from 0 to 315
- list_len: int32 [32], P('grp'), may hold values from 1 to 8
Outputs:
- received: float32 [2, 32, 2, 1, 8192], P(None, 'grp', None, None, 'ang')
All inputs are finite; a program needn't handle non-finite values. No bound on the sum of `present` on one device may be relied on, other than what follows from the above.
Results may differ from a plain program's by a relative error of at most 0.0029.
Values may be sent and summed in bfloat16 or wider, within the bound.
A program may use at most 128 MiB of HBM per device.

v0:
```python
import jax
import jax.numpy as jnp
from jax import lax
from jax.sharding import PartitionSpec as P

HW = 4


def aggregate(extended, weights, cosine, sine_part, coarse_len):
    taps_count = weights.shape[0]
    octants = extended.shape[2]
    fine_len = 4 * coarse_len
    real_acc = None
    imag_acc = None
    for octant in range(octants):
        spread = jnp.repeat(extended[:, :, octant].astype(jnp.float32), 4, axis=-1)
        refined = jnp.zeros(spread.shape[:-1] + (fine_len,), jnp.float32)
        for stencil in range(taps_count):
            window = spread[..., 4 * stencil : 4 * stencil + fine_len]
            refined = refined + window * weights[stencil]
        cos_row = cosine[octant]
        sin_row = sine_part[octant]
        real_term = refined[0] * cos_row - refined[1] * sin_row
        imag_term = refined[0] * sin_row + refined[1] * cos_row
        if real_acc is None:
            real_acc = real_term
            imag_acc = imag_term
        else:
            real_acc = real_acc + real_term
            imag_acc = imag_acc + imag_term
    return jnp.stack([real_acc, imag_acc]).astype(jnp.bfloat16)


def local(children, present, interp, phase, trans, sources, trans_ids, list_len):
    present_mask = present.astype(jnp.bfloat16)[None, :, :, None, None, None]
    kept_children = children * present_mask
    cosine = jnp.cos(phase)
    sine_part = jnp.sin(phase)
    extended = jnp.concatenate(
        [kept_children[..., -HW:], kept_children, kept_children[..., :HW]], axis=-1
    )
    parent_pattern = aggregate(extended, interp, cosine, sine_part, kept_children.shape[-1])
    pattern = lax.all_to_all(parent_pattern, "ang", split_axis=4, concat_axis=1, tiled=True)
    all_patterns = lax.all_gather(pattern, "grp", axis=1, tiled=True)

    def one_slot(position, carried):
        real_sum, imag_sum = carried
        source_ids = lax.dynamic_index_in_dim(sources, position, 1, keepdims=False)
        operator_ids = lax.dynamic_index_in_dim(trans_ids, position, 1, keepdims=False)
        source_rows = jnp.take(all_patterns, source_ids, axis=1).astype(jnp.float32)
        operator_cols = jnp.take(trans, operator_ids, axis=1)[:, :, None, None, :]
        active = (position < list_len).astype(jnp.float32)[:, None, None, None]
        real_sum = real_sum + active * (
            operator_cols[0] * source_rows[0] - operator_cols[1] * source_rows[1]
        )
        imag_sum = imag_sum + active * (
            operator_cols[0] * source_rows[1] + operator_cols[1] * source_rows[0]
        )
        return (real_sum, imag_sum)

    zeros_start = jnp.zeros(pattern.shape[1:], jnp.float32)
    real_sum, imag_sum = lax.fori_loop(0, sources.shape[1], one_slot, (zeros_start, zeros_start))
    return jnp.stack([real_sum, imag_sum])


def solution(mesh):
    return jax.shard_map(
        local,
        mesh=mesh,
        in_specs=(
            P(None, ("grp", "ang"), None, None, None, None),
            P(("grp", "ang"), None),
            P(),
            P(),
            P(None, None, "ang"),
            P("grp", None),
            P("grp", None),
            P("grp"),
        ),
        out_specs=P(None, "grp", None, None, "ang"),
        check_vma=False,
    )
```

profile of v0, /device:TPU:0, one launch (start us, length us, event | category | flops | bytes accessed | tf_op | source)
XLA Modules:
  0.0 148.3 jit_solution(11333741935518741040)
XLA Ops:
  0.0 2.6 %fusion.69 = (f32[1,8192]{1,0:T(1,128)S(1)}, f32[1,8192]{1,0:T(1,128)S(1)}, f32[1,8192]{1,0:T(1,128)S(1)}, f32[1,8192]{1,0:T(1,128)S(1)}, f32[1,8192]{1,0:T(1,12...) fusion(f32[8,8192]{1,0:T(8,128)} %param.12), kind=kLoop, calls=%fused_computation.164 | loop fusion | bytes 524288 | tf_op jit(solution)/shard_map/slice | solution.py:20
  2.6 0.7 convert_bitcast_fusion
  3.3 1.1 broadcast_multiply_fusion
  4.4 0.7 concatenate.12
  5.2 2.6 %broadcast_in_dim.97 = f32[2,2,2056,4]{3,2,1,0:T(8,128)} broadcast(f32[2,2,2056]{2,1,0:T(2,128)S(1)} %get-tuple-element.229), dimensions={0,1,2} | broadcast | bytes 164480 | tf_op jit(solution)/shard_map/broadcast_in_dim | solution.py:16
  7.8 3.6 %broadcast_in_dim.98 = f32[2,1,2,1,8224]{4,2,0,3,1:T(2,128)S(1)} reshape(f32[2,2,2056,4]{3,2,1,0:T(8,128)} %broadcast_in_dim.97) | data formatting | bytes 263168 | tf_op jit(solution)/shard_map/broadcast_in_dim | solution.py:16
  11.4 2.6 %broadcast_in_dim.95 = f32[2,2,2056,4]{3,2,1,0:T(8,128)} broadcast(f32[2,2,2056]{2,1,0:T(2,128)S(1)} %get-tuple-element.230), dimensions={0,1,2} | broadcast | bytes 164480 | tf_op jit(solution)/shard_map/broadcast_in_dim | solution.py:16
  13.9 3.6 %broadcast_in_dim.96 = f32[2,1,2,1,8224]{4,2,0,3,1:T(2,128)S(1)} reshape(f32[2,2,2056,4]{3,2,1,0:T(8,128)} %broadcast_in_dim.95) | data formatting | bytes 263168 | tf_op jit(solution)/shard_map/broadcast_in_dim | solution.py:16
  17.5 1.0 fusion.15
  18.5 1.0 fusion.22
  19.6 2.6 %broadcast_in_dim.93 = f32[2,2,2056,4]{3,2,1,0:T(8,128)} broadcast(f32[2,2,2056]{2,1,0:T(2,128)S(1)} %get-tuple-element.231), dimensions={0,1,2} | broadcast | bytes 164480 | tf_op jit(solution)/shard_map/broadcast_in_dim | solution.py:16
  22.1 3.6 %broadcast_in_dim.94 = f32[2,1,2,1,8224]{4,2,0,3,1:T(2,128)S(1)} reshape(f32[2,2,2056,4]{3,2,1,0:T(8,128)} %broadcast_in_dim.93) | data formatting | bytes 263168 | tf_op jit(solution)/shard_map/broadcast_in_dim | solution.py:16
  25.7 1.0 fusion.29
  26.7 2.6 %broadcast_in_dim.91 = f32[2,2,2056,4]{3,2,1,0:T(8,128)} broadcast(f32[2,2,2056]{2,1,0:T(2,128)S(1)} %get-tuple-element.232), dimensions={0,1,2} | broadcast | bytes 164480 | tf_op jit(solution)/shard_map/broadcast_in_dim | solution.py:16
  29.3 3.6 %broadcast_in_dim.92 = f32[2,1,2,1,8224]{4,2,0,3,1:T(2,128)S(1)} reshape(f32[2,2,2056,4]{3,2,1,0:T(8,128)} %broadcast_in_dim.91) | data formatting | bytes 263168 | tf_op jit(solution)/shard_map/broadcast_in_dim | solution.py:16
  32.9 1.0 fusion.36
  33.9 2.6 %broadcast_in_dim.89 = f32[2,2,2056,4]{3,2,1,0:T(8,128)} broadcast(f32[2,2,2056]{2,1,0:T(2,128)S(1)} %get-tuple-element.233), dimensions={0,1,2} | broadcast | bytes 164480 | tf_op jit(solution)/shard_map/broadcast_in_dim | solution.py:16
  36.5 3.7 %broadcast_in_dim.90 = f32[2,1,2,1,8224]{4,2,0,3,1:T(2,128)S(1)} reshape(f32[2,2,2056,4]{3,2,1,0:T(8,128)} %broadcast_in_dim.89) | data formatting | bytes 263168 | tf_op jit(solution)/shard_map/broadcast_in_dim | solution.py:16
  40.2 1.0 fusion.43
  41.3 2.6 %broadcast_in_dim.87 = f32[2,2,2056,4]{3,2,1,0:T(8,128)} broadcast(f32[2,2,2056]{2,1,0:T(2,128)S(1)} %get-tuple-element.226), dimensions={0,1,2} | broadcast | bytes 164480 | tf_op jit(solution)/shard_map/broadcast_in_dim | solution.py:16
  43.8 3.6 %broadcast_in_dim.88 = f32[2,1,2,1,8224]{4,2,0,3,1:T(2,128)S(1)} reshape(f32[2,2,2056,4]{3,2,1,0:T(8,128)} %broadcast_in_dim.87) | data formatting | bytes 263168 | tf_op jit(solution)/shard_map/broadcast_in_dim | solution.py:16
  47.4 1.0 fusion.50
  48.4 2.6 %broadcast_in_dim.99 = f32[2,2,2056,4]{3,2,1,0:T(8,128)} broadcast(f32[2,2,2056]{2,1,0:T(2,128)S(1)} %get-tuple-element.228), dimensions={0,1,2} | broadcast | bytes 164480 | tf_op jit(solution)/shard_map/broadcast_in_dim | solution.py:16
  51.0 3.6 %broadcast_in_dim.100 = f32[2,1,2,1,8224]{4,2,0,3,1:T(2,128)S(1)} reshape(f32[2,2,2056,4]{3,2,1,0:T(8,128)} %broadcast_in_dim.99) | data formatting | bytes 263168 | tf_op jit(solution)/shard_map/broadcast_in_dim | solution.py:16
  54.6 1.0 fusion.8
  55.6 2.6 %broadcast_in_dim.101 = f32[2,2,2056,4]{3,2,1,0:T(8,128)} broadcast(f32[2,2,2056]{2,1,0:T(2,128)S(1)} %get-tuple-element.227), dimensions={0,1,2} | broadcast | bytes 164480 | tf_op jit(solution)/shard_map/broadcast_in_dim | solution.py:16
  58.2 3.6 %broadcast_in_dim.102 = f32[2,1,2,1,8224]{4,2,0,3,1:T(2,128)S(1)} reshape(f32[2,2,2056,4]{3,2,1,0:T(8,128)} %broadcast_in_dim.101) | data formatting | bytes 263168 | tf_op jit(solution)/shard_map/broadcast_in_dim | solution.py:16
  61.8 1.0 fusion.1
  62.8 1.0 fusion.68
  63.8 0.5 fusion.66
  64.3 0.4 add_convert_fusion.1
  65.2 6.8 %copy.14 = bf16[2,1,2,1,8192]{2,0,3,1,4:T(2,128)(2,1)} copy(bf16[2,1,2,1,8192]{4,2,0,3,1:T(2,128)(2,1)S(1)} %pad_maximum_fusion.1) | data formatting | bytes 131072 | tf_op jit(solution)/shard_map/stack | solution.py:31
  72.0 7.8 %reshape.696 = bf16[16,2,1024]{2,1,0:T(2,128)(2,1)} reshape(bf16[8192,1,1,2,2]{4,3,2,1,0:T(2,128)(2,1)} %bitcast.144) | data formatting | bytes 131072
  79.8 7.4 %all-to-all-start = ((bf16[16,2,1024]{2,1,0:T(2,128)(2,1)}), bf16[16,2,1024]{2,1,0:T(2,128)(2,1)S(1)}, u32[]{:S(2)}, u32[]{:S(2)}) async-start(bf16[16,2,1024]{2,1,0:T(2,128)(2,1)} %reshape.696), calls=%async_computation | async-start | bytes 131072 | tf_op jit(solution)/shard_map/all_to_all | solution.py:43
  87.2 6.9 %all-to-all-done = bf16[16,2,1024]{2,1,0:T(2,128)(2,1)S(1)} async-done(((bf16[16,2,1024]{2,1,0:T(2,128)(2,1)}), bf16[16,2,1024]{2,1,0:T(2,128)(2,1)S(1)}, u32[]{:S(2)}, u32[]{:S(2)}) %all-to-all-start) | async-done | bytes 65568 | tf_op jit(solution)/shard_map/all_to_all | solution.py:43
  94.1 10.0 %reshape.697 = bf16[8192,1,1,2,2]{4,3,2,1,0:T(2,128)(2,1)} reshape(bf16[16,2,1024]{2,1,0:T(2,128)(2,1)S(1)} %all-to-all-done) | data formatting | bytes 131072
  104.1 6.1 %copy.16 = bf16[2,1,2,1,16,512]{5,4,3,2,1,0:T(8,128)(2,1)S(1)} copy(bf16[2,1,2,1,16,512]{2,0,5,4,3,1:T(2,128)(2,1)} %bitcast.145) | data formatting | bytes 131072 | tf_op jit(solution)/shard_map/all_to_all | solution.py:43
  110.2 4.9 %all-gather = bf16[2,32,1,2,1,512]{5,1,4,3,2,0:T(8,128)(2,1)S(1)} all-gather(bf16[2,16,1,2,1,512]{5,1,4,3,2,0:T(8,128)(2,1)S(1)} %bitcast.246), channel_id=2, replica_groups=mesh['grp'=2,'ang'=16] {'grp'}, dimensions={1}, use_global_device_ids=true | all-gather | bytes 196608 | tf_op jit(solution)/shard_map/all_gather | solution.py:44
  115.1 32.2 %while.16 = (s32[]{:T(128)}, f32[16,2,1,512]{3,1,0,2:T(2,128)S(1)}, f32[16,2,1,512]{3,1,0,2:T(2,128)S(1)}, s32[16]{0:T(128)S(1)}, s32[16,8]{0,1:T(8,128)}, /*ind...) while((s32[]{:T(128)}, f32[16,2,1,512]{3,1,0,2:T(2,128)S(1)}, ...), condition=%wide.region_1.2_spmd.clone, body=%wide.region_0.1_spmd.clone.sunk | while | flops 280803 | bytes 1581943 | solution.py:62
  115.1 0.7 and_bitcast_fusion.3
  115.9 1.9 %gather_fusion.1 = f32[16,2,512]{2,1,0:T(2,128)S(1)} fusion(f32[2,316,512]{2,0,1:T(2,128)} %get-tuple-element.334, s32[1024]{0:T(1024)S(1)} %pad_clamp_fusion.5), kind=kCustom, calls=%fused_computation.clone.clone.1 | custom fusion | bytes 131136 | tf_op jit(solution)/shard_map/while/body/eval_jaxpr/jit(_take)/gather | solution.py:51
  118.1 0.7 gather_fusion
  119.2 0.7 and_bitcast_fusion.3
  119.9 1.9 %gather_fusion.1 = f32[16,2,512]{2,1,0:T(2,128)S(1)} fusion(f32[2,316,512]{2,0,1:T(2,128)} %get-tuple-element.334, s32[1024]{0:T(1024)S(1)} %pad_clamp_fusion.5), kind=kCustom, calls=%fused_computation.clone.clone.1 | custom fusion | bytes 131136 | tf_op jit(solution)/shard_map/while/body/eval_jaxpr/jit(_take)/gather | solution.py:51
  122.2 0.7 gather_fusion
  123.2 0.7 and_bitcast_fusion.3
  123.9 1.9 %gather_fusion.1 = f32[16,2,512]{2,1,0:T(2,128)S(1)} fusion(f32[2,316,512]{2,0,1:T(2,128)} %get-tuple-element.334, s32[1024]{0:T(1024)S(1)} %pad_clamp_fusion.5), kind=kCustom, calls=%fused_computation.clone.clone.1 | custom fusion | bytes 131136 | tf_op jit(solution)/shard_map/while/body/eval_jaxpr/jit(_take)/gather | solution.py:51
  126.2 0.7 gather_fusion
  127.2 0.7 and_bitcast_fusion.3
  128.0 1.9 %gather_fusion.1 = f32[16,2,512]{2,1,0:T(2,128)S(1)} fusion(f32[2,316,512]{2,0,1:T(2,128)} %get-tuple-element.334, s32[1024]{0:T(1024)S(1)} %pad_clamp_fusion.5), kind=kCustom, calls=%fused_computation.clone.clone.1 | custom fusion | bytes 131136 | tf_op jit(solution)/shard_map/while/body/eval_jaxpr/jit(_take)/gather | solution.py:51
  130.2 0.7 gather_fusion
  131.3 0.7 and_bitcast_fusion.3
  132.0 1.9 %gather_fusion.1 = f32[16,2,512]{2,1,0:T(2,128)S(1)} fusion(f32[2,316,512]{2,0,1:T(2,128)} %get-tuple-element.334, s32[1024]{0:T(1024)S(1)} %pad_clamp_fusion.5), kind=kCustom, calls=%fused_computation.clone.clone.1 | custom fusion | bytes 131136 | tf_op jit(solution)/shard_map/while/body/eval_jaxpr/jit(_take)/gather | solution.py:51
  134.3 0.7 gather_fusion
  135.3 0.7 and_bitcast_fusion.3
  136.0 1.9 %gather_fusion.1 = f32[16,2,512]{2,1,0:T(2,128)S(1)} fusion(f32[2,316,512]{2,0,1:T(2,128)} %get-tuple-element.334, s32[1024]{0:T(1024)S(1)} %pad_clamp_fusion.5), kind=kCustom, calls=%fused_computation.clone.clone.1 | custom fusion | bytes 131136 | tf_op jit(solution)/shard_map/while/body/eval_jaxpr/jit(_take)/gather | solution.py:51
  138.3 0.7 gather_fusion
  139.3 0.7 and_bitcast_fusion.3
  140.0 1.9 %gather_fusion.1 = f32[16,2,512]{2,1,0:T(2,128)S(1)} fusion(f32[2,316,512]{2,0,1:T(2,128)} %get-tuple-element.334, s32[1024]{0:T(1024)S(1)} %pad_clamp_fusion.5), kind=kCustom, calls=%fused_computation.clone.clone.1 | custom fusion | bytes 131136 | tf_op jit(solution)/shard_map/while/body/eval_jaxpr/jit(_take)/gather | solution.py:51
  142.3 0.7 gather_fusion
  143.3 0.7 and_bitcast_fusion.3
  144.1 1.9 %gather_fusion.1 = f32[16,2,512]{2,1,0:T(2,128)S(1)} fusion(f32[2,316,512]{2,0,1:T(2,128)} %get-tuple-element.334, s32[1024]{0:T(1024)S(1)} %pad_clamp_fusion.5), kind=kCustom, calls=%fused_computation.clone.clone.1 | custom fusion | bytes 131136 | tf_op jit(solution)/shard_map/while/body/eval_jaxpr/jit(_take)/gather | solution.py:51
  146.4 0.7 gather_fusion
  147.5 0.8 pad_maximum_fusion
  (92 shorter events, 5.6 us)
Async XLA Ops:
  55.6 7.2 %copy-start = (f32[8,8192]{1,0:T(8,128)S(1)}, f32[8,8192]{1,0:T(8,128)}, u32[]{:S(2)}) copy-start(f32[8,8192]{1,0:T(8,128)} %param.13) | copy-start | bytes 786436
  79.8 14.3 %all-to-all-start = ((bf16[16,2,1024]{2,1,0:T(2,128)(2,1)}), bf16[16,2,1024]{2,1,0:T(2,128)(2,1)S(1)}, u32[]{:S(2)}, u32[]{:S(2)}) async-start(bf16[16,2,1024]{2,1,0:T(2,128)(2,1)} %reshape.696), calls=%async_computation | async-start | bytes 131072 | tf_op jit(solution)/shard_map/all_to_all | solution.py:43
  87.2 27.9 %copy-start.1 = (s32[16]{0:T(128)S(1)}, s32[16]{0:T(128)}, u32[]{:S(2)}) copy-start(s32[16]{0:T(128)} %param.17) | copy-start | bytes 196
where the time goes:
time: 149 us; the launch traced here: 148 us
  local copies, waits for them, and re-layouts  108 us (72%)
  other arithmetic  20.6 us (14%)
  starting transfers between devices  7.39 us (5%)
  waiting for transfers between devices  6.86 us (5%)
  blocking collectives  4.94 us (3%)
    broadcast_in_dim x16, local copies, waits for them, and re-layouts, aggregate(): spread = jnp.repeat(extended[:, :, octant].astype(jnp.float32), 4, axis=-1)  49.3 us
    unnamed x6, local copies, waits for them, and re-layouts  17.8 us
    gather x8, local copies, waits for them, and re-layouts, one_slot(): operator_cols = jnp.take(trans, operator_ids, axis=1)[:, :, None, None, :]  15.5 us
    add x8, other arithmetic, aggregate(): refined = refined + window * weights[stencil]  8.14 us
    all_to_all x1, starting transfers between devices, local(): lax.all_to_all(parent_pattern, 'ang', split_axis=4, concat_axis=1, tiled=...  7.39 us
    all_to_all x1, waiting for transfers between devices, local(): lax.all_to_all(parent_pattern, 'ang', split_axis=4, concat_axis=1, tiled=...  6.86 us
    another operation x1, local copies, waits for them, and re-layouts, aggregate(): return jnp.stack([real_acc, imag_acc]).astype(jnp.bfloat16)  6.84 us
    all_to_all x1, local copies, waits for them, and re-layouts, local(): lax.all_to_all(parent_pattern, 'ang', split_axis=4, concat_axis=1, tiled=...  6.1 us
  transfers between devices with their start and end apart: 1, of which 1 were waited for; matrix products, arithmetic and copies ran while one was open for 0% of the time, Pallas kernels for 0%

commit v1 on v0

v1 whole, which is shorter than its diff:
```python
import functools

import jax
import jax.numpy as jnp
from jax import lax
from jax.experimental import pallas as pl
from jax.experimental.pallas import tpu as pltpu
from jax.sharding import PartitionSpec as P

MESH = pl.DeviceIdType.MESH
F32, BF16 = jnp.float32, jnp.bfloat16
LANES, SUBS = 128, 8

SIN_COEFFS = (1.0, -1.0 / 6, 1.0 / 120, -1.0 / 5040, 1.0 / 362880, -1.0 / 39916800)
COS_COEFFS = (1.0, -1.0 / 2, 1.0 / 24, -1.0 / 720, 1.0 / 40320, -1.0 / 3628800, 1.0 / 479001600)


def horner(coeffs, x):
    total = jnp.full_like(x, coeffs[-1])
    for coeff in coeffs[-2::-1]:
        total = total * x + coeff
    return total


def sin_cos(angle):
    half = angle * 0.5
    square = half * half
    sine = half * horner(SIN_COEFFS, square)
    cosine = horner(COS_COEFFS, square)
    return 2.0 * sine * cosine, 1.0 - 2.0 * sine * sine


def iota(shape, axis):
    return lax.broadcasted_iota(jnp.int32, shape, axis)


def sublane_sums(rows, sub):
    low = (sub & 4) == 0
    rows = [
        jnp.where(low, rows[i], rows[i + 4]) + pltpu.roll(jnp.where(low, rows[i + 4], rows[i]), 4, 0)
        for i in range(4)
    ]
    for step in (2, 1):
        low = (sub & step) == 0
        rows = [
            jnp.where(low, rows[i], rows[i + step])
            + jnp.where(low, pltpu.roll(rows[i], SUBS - step, 0), pltpu.roll(rows[i + step], step, 0))
            for i in range(step)
        ]
    return rows[0]


def kernel(
    grp_size, ang_size, unroll,
    children, present, interp, phase, trans, sources, trans_ids, list_len,
    out,
    child_v, interp_v, phase_v, trans_v, slabs, lhs, send, recv, picked, patterns, turned,
    load_sems, send_sem, recv_sem,
):
    my_grp, my_ang = lax.axis_index("grp"), lax.axis_index("ang")
    devices = grp_size * ang_size
    me = my_grp * ang_size + my_ang

    loads = [
        pltpu.make_async_copy(src, dst, load_sems.at[i])
        for i, (src, dst) in enumerate(
            ((children, child_v), (interp, interp_v), (phase, phase_v), (trans, trans_v))
        )
    ]
    for load in loads:
        load.start()

    barrier = pltpu.get_barrier_semaphore()

    def greet(step, carry):
        other = lax.rem(me + step, devices)
        pl.semaphore_signal(
            barrier, inc=1, device_id=(other // ang_size, lax.rem(other, ang_size)), device_id_type=MESH
        )
        return carry

    lax.fori_loop(1, devices, greet, 0)

    sub = iota((SUBS, LANES), 0)
    octants = present.shape[1]
    mask = jnp.zeros((SUBS, LANES), F32)
    for octant in range(octants):
        mask = jnp.where(sub == octant, present[0, octant].astype(F32), mask)

    loads[0].wait()
    coarse_tiles = slabs.shape[0]
    for tile in range(coarse_tiles):
        part = child_v[:, :, tile * LANES:(tile + 1) * LANES].astype(F32)
        for row in range(part.shape[0]):
            slabs[tile, 2 * row:2 * row + 2, :] = part[row]
    half_width = interp.shape[0] // 2
    lane = iota((SUBS, LANES), 1)

    def shifted(here, before, by):
        return jnp.where(lane < by, pltpu.roll(before, by, 1), pltpu.roll(here, by, 1))

    for pol in range(2):
        groups = []
        for reim in range(2):
            tiles = [
                slabs[tile, pl.ds(2 * octants * reim + pol, octants, stride=2), :] * mask
                for tile in range(coarse_tiles)
            ]
            groups.append(tiles)
        for tile in range(coarse_tiles):
            first = [shifted(g[tile], g[tile - 1], half_width) for g in groups]
            second = [
                shifted(g[(tile + 1) % coarse_tiles], g[tile], half_width + LANES // 2) for g in groups
            ]
            rows = slice(2 * octants * pol, 2 * octants * (pol + 1))
            lhs[tile, 0, rows, :] = jnp.concatenate(first, axis=0).astype(BF16)
            lhs[tile, 1, rows, :] = jnp.concatenate(second, axis=0).astype(BF16)

    loads[1].wait()
    loads[2].wait()

    band_rows = 48
    gap = iota((band_rows, LANES), 0) - iota((band_rows, LANES), 1) // 4
    band = jnp.where((gap >= 0) & (gap < SUBS), 1.0, 0.0).astype(BF16)
    turn = lane // 4

    def banded(weights):
        for step in (1, 2, 4):
            weights = jnp.where((turn & step) != 0, pltpu.roll(weights, step, 0), weights)
        high = weights.astype(BF16)
        low = (weights - high.astype(F32)).astype(BF16)
        return [jnp.concatenate([x] * (band_rows // SUBS), axis=0) * band for x in (high, low)]

    def blank(rows):
        return jnp.zeros((rows, LANES), BF16)

    def one_block(block):
        real, imag = [], []
        for half in range(2):
            x = lhs[block, half]
            cols = []
            for tile in range(2):
                at = pl.multiple_of((4 * block + 2 * half + tile) * LANES, LANES)
                pieces = []
                for piece in banded(interp_v[:, pl.ds(at, LANES)]):
                    pieces += [blank(32 * tile), piece] if tile else [piece]
                    pieces.append(blank(LANES - band_rows - 32 * tile))
                cols.append(jnp.concatenate(pieces, axis=0))
            fine = jnp.dot(
                jnp.concatenate([x, x], axis=1), jnp.concatenate(cols, axis=1), preferred_element_type=F32
            )
            for tile in range(2):
                at = pl.multiple_of((4 * block + 2 * half + tile) * LANES, LANES)
                sine, cosine = sin_cos(phase_v[:, pl.ds(at, LANES)])
                for pol in range(2):
                    re = fine[16 * pol:16 * pol + 8, tile * LANES:(tile + 1) * LANES]
                    im = fine[16 * pol + 8:16 * pol + 16, tile * LANES:(tile + 1) * LANES]
                    real.append(re * cosine - im * sine)
                    imag.append(re * sine + im * cosine)
        return jnp.concatenate([sublane_sums(real, sub), sublane_sums(imag, sub)], axis=0).astype(BF16)

    def post(block):
        for step in range(grp_size):
            grp = lax.rem(my_grp + step, grp_size)

            def away():
                pltpu.make_async_remote_copy(
                    src_ref=send.at[block], dst_ref=recv.at[me], send_sem=send_sem, recv_sem=recv_sem,
                    device_id=(grp, block), device_id_type=MESH,
                ).start()

            if step:
                away()
            else:
                pl.when(block != my_ang)(away)

                @pl.when(block == my_ang)
                def _():
                    pltpu.make_async_copy(send.at[block], recv.at[me], recv_sem).start()

    def blocks_of(step):
        return [lax.rem(my_ang + 1 + step * unroll + i, ang_size) for i in range(unroll)]

    def aggregate(step):
        for block in blocks_of(step):
            send[block] = one_block(block)

    def dispatch(step):
        for block in blocks_of(step):
            post(block)

    aggregate(0)
    pl.semaphore_wait(barrier, devices - 1)
    dispatch(0)

    def advance(step, carry):
        aggregate(step)
        dispatch(step)
        return carry

    lax.fori_loop(1, ang_size // unroll, advance, 0)

    loads[3].wait()
    slots, clusters = sources.shape
    even = (sub & 1) == 0

    def pick(cluster, carry):
        for slot in range(slots):
            both = trans_v[trans_ids[slot, cluster]]
            both = both * jnp.where(slot < list_len[cluster], 1.0, 0.0)
            picked[cluster * slots + slot, 0] = jnp.where(even, both, pltpu.roll(both, 1, 0))
            picked[cluster * slots + slot, 1] = jnp.where(even, pltpu.roll(both, SUBS - 1, 0), both)
        return carry

    lax.fori_loop(0, clusters, pick, 0, unroll=2)

    pltpu.make_async_copy(recv, recv, recv_sem).wait()

    def widen(source, carry):
        patterns[source] = recv[source].astype(F32)
        return carry

    lax.fori_loop(0, devices, widen, 0, unroll=8)

    def receive(cluster, carry):
        real = imag = jnp.zeros((SUBS, LANES), F32)
        for slot in range(slots):
            source = sources[slot, cluster]
            row = cluster * slots + slot
            op_re, op_im = picked[row, 0], picked[row, 1]
            src_re, src_im = patterns[source, 0:SUBS], patterns[source, SUBS:2 * SUBS]
            real += op_re * src_re - op_im * src_im
            imag += op_re * src_im + op_im * src_re
        for part, value in enumerate((real, imag)):
            turned[cluster, part] = value
            for pol in range(2):
                out[part, cluster, 4 * pol:4 * pol + 4, :] = turned[cluster, part, pl.ds(pol, 4, stride=2), :]
        return carry

    lax.fori_loop(0, clusters, receive, 0, unroll=2)

    sent = recv.at[pl.ds(0, devices - 1)]
    pltpu.make_async_copy(sent, sent, send_sem).wait()


def local(grp_size, ang_size, children, present, interp, phase, trans, sources, trans_ids, list_len):
    parts, own, octants, pols, angles, coarse = children.shape
    operators, width = trans.shape[1:]
    clusters, slots = sources.shape
    devices = grp_size * ang_size
    quarters = width // LANES
    assert (parts, own, octants, pols, angles, quarters) == (2, 1, SUBS, 2, 1, 4)
    assert interp.shape[0] == SUBS and interp.shape[1] == ang_size * width == 4 * coarse
    children = children.reshape(parts * octants, pols, coarse)
    trans = trans.transpose(1, 0, 2).reshape(operators, parts, quarters, LANES)
    trans = trans.transpose(0, 2, 1, 3).reshape(operators, quarters * parts, LANES)
    anywhere = pl.BlockSpec(memory_space=pl.ANY)
    scalars = pl.BlockSpec(memory_space=pltpu.SMEM)
    tile_rows = 2 * SUBS
    received = pl.pallas_call(
        functools.partial(kernel, grp_size, ang_size, 4),
        out_shape=jax.ShapeDtypeStruct((parts, clusters, SUBS, LANES), F32),
        in_specs=[anywhere, scalars, anywhere, anywhere, anywhere, scalars, scalars, scalars],
        out_specs=pl.BlockSpec(memory_space=pltpu.VMEM),
        scratch_shapes=[
            pltpu.VMEM(children.shape, BF16),
            pltpu.VMEM(interp.shape, F32),
            pltpu.VMEM(phase.shape, F32),
            pltpu.VMEM(trans.shape, F32),
            pltpu.VMEM((coarse // LANES, parts * octants * pols, LANES), F32),
            pltpu.VMEM((coarse // LANES, 2, parts * octants * pols, LANES), BF16),
            pltpu.VMEM((ang_size, tile_rows, LANES), BF16),
            pltpu.VMEM((devices, tile_rows, LANES), BF16),
            pltpu.VMEM((clusters * slots, 2, SUBS, LANES), F32),
            pltpu.VMEM((devices, tile_rows, LANES), F32),
            pltpu.VMEM((clusters, 2, SUBS, LANES), F32),
            pltpu.SemaphoreType.DMA((4,)),
            pltpu.SemaphoreType.DMA,
            pltpu.SemaphoreType.DMA,
        ],
        compiler_params=pltpu.CompilerParams(
            collective_id=0, has_side_effects=True, vmem_limit_bytes=48 * 1024 * 1024
        ),
    )(children, present, interp, phase, trans, sources.T, trans_ids.T, list_len)
    return received.reshape(parts, clusters, pols, angles, width)


def solution(mesh):
    return jax.shard_map(
        functools.partial(local, mesh.shape["grp"], mesh.shape["ang"]),
        mesh=mesh,
        in_specs=(
            P(None, ("grp", "ang"), None, None, None, None),
            P(("grp", "ang"), None),
            P(),
            P(),
            P(None, None, "ang"),
            P("grp", None),
            P("grp", None),
            P("grp"),
        ),
        out_specs=P(None, "grp", None, None, "ang"),
        check_vma=False,
    )
```

time: 149 us -> 20.2 us (0.14)
  local copies, waits for them, and re-layouts: 108 us -> 7.45 us
  other arithmetic: 20.6 us -> 0 us
  Pallas kernels: 0 us -> 12.4 us
  starting transfers between devices: 7.39 us -> 0 us
  waiting for transfers between devices: 6.86 us -> 0 us
  blocking collectives: 4.94 us -> 0 us
    broadcast_in_dim x16 -> x0, local copies, waits for them, and re-layouts: 49.3 us -> none  [aggregate(): spread = jnp.repeat(extended[:, :, octant].astype(jnp.float32), 4, axis=-1)]
    gather x16 -> x0, local copies, waits for them, and re-layouts: 21 us -> none  [the longest x8 15.5 us: one_slot(): operator_cols = jnp.take(trans, operator_ids, axis=1)[:, :, None, None, :]]
    pallas_call x0 -> x1, Pallas kernels: none -> 12.4 us  [local(): pl.pallas_call(functools.partial(kernel, grp_size, ang_size, 4), out_shap...]
    unnamed x6 -> x17, local copies, waits for them, and re-layouts: 17.8 us -> 7.45 us
    add x16 -> x0, other arithmetic: 9.52 us -> none  [the longest x8 8.14 us: aggregate(): refined = refined + window * weights[stencil]]
    another operation x11 -> x0, local copies, waits for them, and re-layouts: 8.03 us -> none  [the longest x1 6.84 us: aggregate(): return jnp.stack([real_acc, imag_acc]).astype(jnp.bfloat16)]
    all_to_all x1 -> x0, starting transfers between devices: 7.39 us -> none  [local(): lax.all_to_all(parent_pattern, 'ang', split_axis=4, concat_axis=1, tiled=...]
    all_to_all x1 -> x0, waiting for transfers between devices: 6.86 us -> none  [local(): lax.all_to_all(parent_pattern, 'ang', split_axis=4, concat_axis=1, tiled=...]
  transfers between devices with their start and end apart: 1 -> 0, of which waited for: 1 -> 0; matrix products, arithmetic and copies ran while one was open for 0% -> 0% of each run, Pallas kernels for 0% -> 0%
where the time goes in v1:
time: 20.2 us; the launch traced here: 19.9 us
  Pallas kernels  12.4 us (61%)
  local copies, waits for them, and re-layouts  7.45 us (37%)
    pallas_call x1, Pallas kernels, local(): pl.pallas_call(functools.partial(kernel, grp_size, ang_size, 4), out_shap...  12.4 us
    unnamed x17, local copies, waits for them, and re-layouts  7.45 us

profile of v1, /device:TPU:0, one launch (start us, length us, event | category | flops | bytes accessed | tf_op | source)
XLA Modules:
  0.0 19.9 jit_solution(10978216783563237651)
XLA Ops:
  0.0 0.0 copy-start
  0.0 1.3 %copy-done = f32[2,316,512]{2,0,1:T(2,128)S(1)} copy-done((f32[2,316,512]{2,0,1:T(2,128)S(1)}, f32[2,316,512]{2,0,1:T(2,128)}, u32[]{:S(2)}) %copy-start) | copy-done | bytes 1294360
  1.3 0.0 copy-start.1
  1.3 0.9 %copy-done.1 = f32[8,8192]{1,0:T(8,128)S(1)} copy-done((f32[8,8192]{1,0:T(8,128)S(1)}, f32[8,8192]{1,0:T(8,128)}, u32[]{:S(2)}) %copy-start.1) | copy-done | bytes 262168
  2.3 0.0 copy-start.2
  2.3 0.9 %copy-done.2 = f32[8,8192]{1,0:T(8,128)S(1)} copy-done((f32[8,8192]{1,0:T(8,128)S(1)}, f32[8,8192]{1,0:T(8,128)}, u32[]{:S(2)}) %copy-start.2) | copy-done | bytes 262168
  3.2 0.0 copy-start.3
  3.2 0.9 %copy-done.3 = bf16[2,1,8,2,1,2048]{5,3,4,2,1,0:T(2,128)(2,1)S(1)} copy-done((bf16[2,1,8,2,1,2048]{5,3,4,2,1,0:T(2,128)(2,1)S(1)}, bf16[2,1,8,2,1,2048]{5,3,4,2,1,0:T(2,128)(2,1)}, u32[]{:S(2)}) %copy-start.3) | copy-done | bytes 131096
  4.1 0.0 copy-start.4
  4.1 0.7 %copy-done.4 = s32[16,8]{0,1:T(8,128)S(1)} copy-done((s32[16,8]{0,1:T(8,128)S(1)}, s32[16,8]{0,1:T(8,128)}, u32[]{:S(2)}) %copy-start.4) | copy-done | bytes 536
  4.8 0.0 copy-start.5
  4.8 0.7 %copy-done.5 = s32[16,8]{0,1:T(8,128)S(1)} copy-done((s32[16,8]{0,1:T(8,128)S(1)}, s32[16,8]{0,1:T(8,128)}, u32[]{:S(2)}) %copy-start.5) | copy-done | bytes 536
  5.5 0.0 copy-start.6
  5.5 0.7 %copy-done.6 = s32[1,8]{1,0:T(1,128)S(1)} copy-done((s32[1,8]{1,0:T(1,128)S(1)}, s32[1,8]{1,0:T(1,128)}, u32[]{:S(2)}) %copy-start.6) | copy-done | bytes 56
  6.1 0.0 copy-start.7
  6.2 0.7 %copy-done.7 = s32[16]{0:T(128)S(1)} copy-done((s32[16]{0:T(128)S(1)}, s32[16]{0:T(128)}, u32[]{:S(2)}) %copy-start.7) | copy-done | bytes 88
  6.8 12.4 %shard_map.82 = f32[2,16,8,128]{3,2,1,0:T(8,128)S(1)} custom-call(bf16[16,2,2048]{2,1,0:T(2,128)(2,1)S(1)} %bitcast.13, s32[1,8]{1,0:T(1,128)S(1)} %copy-done.6, f32[8,8192]{1,0:T(8,128)S(1)} %copy-done.1, f32[8,8192]{1,0:T(8,128)S(1)} %copy-done.2, f32[316,8,128]{2,1,0:T(8,128)S(1)} %bitcast.11, s32[8,16]{1,0:T(8,128)S(1)} %bitcast.14, ...), custom_call_target="tpu_custom_call" | custom-call | tf_op jit(solution)/shard_map/pallas_call | solution.py:260
  19.2 0.7 %copy.12 = f32[2,16,2,1,512]{4,3,2,1,0:T(1,128)} copy(f32[2,16,2,1,512]{4,3,2,1,0:T(1,128)S(1)} %bitcast.12) | data formatting | bytes 262144
Async XLA Ops:
  0.0 1.3 %copy-start = (f32[2,316,512]{2,0,1:T(2,128)S(1)}, f32[2,316,512]{2,0,1:T(2,128)}, u32[]{:S(2)}) copy-start(f32[2,316,512]{2,0,1:T(2,128)} %param.12) | copy-start | bytes 3883012
  1.3 0.9 %copy-start.1 = (f32[8,8192]{1,0:T(8,128)S(1)}, f32[8,8192]{1,0:T(8,128)}, u32[]{:S(2)}) copy-start(f32[8,8192]{1,0:T(8,128)} %interp.1) | copy-start | bytes 786436
  2.3 0.9 %copy-start.2 = (f32[8,8192]{1,0:T(8,128)S(1)}, f32[8,8192]{1,0:T(8,128)}, u32[]{:S(2)}) copy-start(f32[8,8192]{1,0:T(8,128)} %phase.1) | copy-start | bytes 786436
  3.2 0.9 %copy-start.3 = (bf16[2,1,8,2,1,2048]{5,3,4,2,1,0:T(2,128)(2,1)S(1)}, bf16[2,1,8,2,1,2048]{5,3,4,2,1,0:T(2,128)(2,1)}, u32[]{:S(2)}) copy-start(bf16[2,1,8,2,1,2048]{5,3,4,2,1,0:T(2,128)(2,1)} %param.8) | copy-start | bytes 393220
  4.1 0.7 %copy-start.4 = (s32[16,8]{0,1:T(8,128)S(1)}, s32[16,8]{0,1:T(8,128)}, u32[]{:S(2)}) copy-start(s32[16,8]{0,1:T(8,128)} %param.13) | copy-start | bytes 1540
  4.8 0.7 %copy-start.5 = (s32[16,8]{0,1:T(8,128)S(1)}, s32[16,8]{0,1:T(8,128)}, u32[]{:S(2)}) copy-start(s32[16,8]{0,1:T(8,128)} %param.14) | copy-start | bytes 1540
  5.5 0.7 %copy-start.6 = (s32[1,8]{1,0:T(1,128)S(1)}, s32[1,8]{1,0:T(1,128)}, u32[]{:S(2)}) copy-start(s32[1,8]{1,0:T(1,128)} %present.1) | copy-start | bytes 100
  6.1 0.7 %copy-start.7 = (s32[16]{0:T(128)S(1)}, s32[16]{0:T(128)}, u32[]{:S(2)}) copy-start(s32[16]{0:T(128)} %list_len.1) | copy-start | bytes 196

commit v2 on v1

--- a/solution.py
+++ b/solution.py
@@ -52,21 +52,20 @@
 
 def kernel(
     grp_size, ang_size, unroll,
-    children, present, interp, phase, trans, sources, trans_ids, list_len,
+    children_h, present_h, interp_h, phase_h, trans_h, sources_h, trans_ids_h, list_len_h,
     out,
-    child_v, interp_v, phase_v, trans_v, slabs, lhs, send, recv, picked, patterns, turned,
+    child_v, present, interp, phase, trans, sources, trans_ids, list_len, slabs, lhs, send, recv, picked, patterns, turned,
     load_sems, send_sem, recv_sem,
 ):
     my_grp, my_ang = lax.axis_index("grp"), lax.axis_index("ang")
     devices = grp_size * ang_size
     me = my_grp * ang_size + my_ang
 
-    loads = [
-        pltpu.make_async_copy(src, dst, load_sems.at[i])
-        for i, (src, dst) in enumerate(
-            ((children, child_v), (interp, interp_v), (phase, phase_v), (trans, trans_v))
-        )
-    ]
+    pairs = (
+        (children_h, child_v), (present_h, present), (interp_h, interp), (phase_h, phase),
+        (trans_h, trans), (sources_h, sources), (trans_ids_h, trans_ids), (list_len_h, list_len),
+    )
+    loads = [pltpu.make_async_copy(src, dst, load_sems.at[i]) for i, (src, dst) in enumerate(pairs)]
     for load in loads:
         load.start()
 
@@ -81,13 +80,14 @@
 
     lax.fori_loop(1, devices, greet, 0)
 
+    loads[0].wait()
+    loads[1].wait()
     sub = iota((SUBS, LANES), 0)
     octants = present.shape[1]
     mask = jnp.zeros((SUBS, LANES), F32)
     for octant in range(octants):
         mask = jnp.where(sub == octant, present[0, octant].astype(F32), mask)
 
-    loads[0].wait()
     coarse_tiles = slabs.shape[0]
     for tile in range(coarse_tiles):
         part = child_v[:, :, tile * LANES:(tile + 1) * LANES].astype(F32)
@@ -116,8 +116,8 @@
             lhs[tile, 0, rows, :] = jnp.concatenate(first, axis=0).astype(BF16)
             lhs[tile, 1, rows, :] = jnp.concatenate(second, axis=0).astype(BF16)
 
-    loads[1].wait()
     loads[2].wait()
+    loads[3].wait()
 
     band_rows = 48
     gap = iota((band_rows, LANES), 0) - iota((band_rows, LANES), 1) // 4
@@ -142,7 +142,7 @@
             for tile in range(2):
                 at = pl.multiple_of((4 * block + 2 * half + tile) * LANES, LANES)
                 pieces = []
-                for piece in banded(interp_v[:, pl.ds(at, LANES)]):
+                for piece in banded(interp[:, pl.ds(at, LANES)]):
                     pieces += [blank(32 * tile), piece] if tile else [piece]
                     pieces.append(blank(LANES - band_rows - 32 * tile))
                 cols.append(jnp.concatenate(pieces, axis=0))
@@ -151,7 +151,7 @@
             )
             for tile in range(2):
                 at = pl.multiple_of((4 * block + 2 * half + tile) * LANES, LANES)
-                sine, cosine = sin_cos(phase_v[:, pl.ds(at, LANES)])
+                sine, cosine = sin_cos(phase[:, pl.ds(at, LANES)])
                 for pol in range(2):
                     re = fine[16 * pol:16 * pol + 8, tile * LANES:(tile + 1) * LANES]
                     im = fine[16 * pol + 8:16 * pol + 16, tile * LANES:(tile + 1) * LANES]
@@ -200,13 +200,14 @@
 
     lax.fori_loop(1, ang_size // unroll, advance, 0)
 
-    loads[3].wait()
+    for load in loads[4:]:
+        load.wait()
     slots, clusters = sources.shape
     even = (sub & 1) == 0
 
     def pick(cluster, carry):
         for slot in range(slots):
-            both = trans_v[trans_ids[slot, cluster]]
+            both = trans[trans_ids[slot, cluster]]
             both = both * jnp.where(slot < list_len[cluster], 1.0, 0.0)
             picked[cluster * slots + slot, 0] = jnp.where(even, both, pltpu.roll(both, 1, 0))
             picked[cluster * slots + slot, 1] = jnp.where(even, pltpu.roll(both, SUBS - 1, 0), both)
@@ -254,19 +255,18 @@
     children = children.reshape(parts * octants, pols, coarse)
     trans = trans.transpose(1, 0, 2).reshape(operators, parts, quarters, LANES)
     trans = trans.transpose(0, 2, 1, 3).reshape(operators, quarters * parts, LANES)
-    anywhere = pl.BlockSpec(memory_space=pl.ANY)
-    scalars = pl.BlockSpec(memory_space=pltpu.SMEM)
+    operands = (children, present, interp, phase, trans, sources.T, trans_ids.T, list_len)
     tile_rows = 2 * SUBS
     received = pl.pallas_call(
         functools.partial(kernel, grp_size, ang_size, 4),
         out_shape=jax.ShapeDtypeStruct((parts, clusters, SUBS, LANES), F32),
-        in_specs=[anywhere, scalars, anywhere, anywhere, anywhere, scalars, scalars, scalars],
+        in_specs=[pl.BlockSpec(memory_space=pltpu.HBM)] * len(operands),
         out_specs=pl.BlockSpec(memory_space=pltpu.VMEM),
         scratch_shapes=[
-            pltpu.VMEM(children.shape, BF16),
-            pltpu.VMEM(interp.shape, F32),
-            pltpu.VMEM(phase.shape, F32),
-            pltpu.VMEM(trans.shape, F32),
+            *(
+                (pltpu.SMEM if operand.dtype == jnp.int32 else pltpu.VMEM)(operand.shape, operand.dtype)
+                for operand in operands
+            ),
             pltpu.VMEM((coarse // LANES, parts * octants * pols, LANES), F32),
             pltpu.VMEM((coarse // LANES, 2, parts * octants * pols, LANES), BF16),
             pltpu.VMEM((ang_size, tile_rows, LANES), BF16),
@@ -274,14 +274,14 @@
             pltpu.VMEM((clusters * slots, 2, SUBS, LANES), F32),
             pltpu.VMEM((devices, tile_rows, LANES), F32),
             pltpu.VMEM((clusters, 2, SUBS, LANES), F32),
-            pltpu.SemaphoreType.DMA((4,)),
+            pltpu.SemaphoreType.DMA((len(operands),)),
             pltpu.SemaphoreType.DMA,
             pltpu.SemaphoreType.DMA,
         ],
         compiler_params=pltpu.CompilerParams(
-            collective_id=0, has_side_effects=True, vmem_limit_bytes=48 * 1024 * 1024
+            collective_id=0, has_side_effects=True, vmem_limit_bytes=60 * 1024 * 1024
         ),
-    )(children, present, interp, phase, trans, sources.T, trans_ids.T, list_len)
+    )(*operands)
     return received.reshape(parts, clusters, pols, angles, width)
 
 

time: 20.2 us -> 13.5 us (0.67); the launches traced: 19.9 us -> 13.4 us
  local copies, waits for them, and re-layouts: 7.45 us -> 1.57 us
  Pallas kernels: 12.4 us -> 11.8 us
    unnamed x17 -> x1, local copies, waits for them, and re-layouts: 7.45 us -> 1.57 us
    pallas_call x1, Pallas kernels: 12.4 us -> 11.8 us  [local(): pl.pallas_call(functools.partial(kernel, grp_size, ang_size, 4), out_shap...]
where the time goes in v2:
time: 13.5 us; the launch traced here: 13.4 us
  Pallas kernels  11.8 us (87%)
  local copies, waits for them, and re-layouts  1.57 us (12%)
    pallas_call x1, Pallas kernels, local(): pl.pallas_call(functools.partial(kernel, grp_size, ang_size, 4), out_shap...  11.8 us
    unnamed x1, local copies, waits for them, and re-layouts  1.57 us

profile of v2, /device:TPU:0, one launch (start us, length us, event | category | flops | bytes accessed | tf_op | source)
XLA Modules:
  0.0 13.4 jit_solution(482340381303597773)
XLA Ops:
  0.0 11.8 %shard_map.82 = f32[2,16,8,128]{3,2,1,0:T(8,128)} custom-call(bf16[16,2,2048]{2,1,0:T(2,128)(2,1)} %bitcast.13, s32[1,8]{1,0:T(1,128)} %present_h.1, f32[8,8192]{1,0:T(8,128)} %interp_h.1, f32[8,8192]{1,0:T(8,128)} %phase_h.1, f32[316,8,128]{2,1,0:T(8,128)} %bitcast.11, s32[8,16]{1,0:T(8,128)} %bitcast.14, s32[8,16]{1,0:T(8,128)} %bitcast.15, s32[16]{0:T(128)} %list_len_h.1), custom_call_target="tpu_custom_call" | custom-call | tf_op jit(solution)/shard_map/pallas_call | solution.py:260
  11.8 1.6 %copy.12 = f32[2,16,2,1,512]{4,3,2,1,0:T(1,128)} copy(f32[2,16,2,1,512]{4,3,2,1,0:T(1,128)} %bitcast.12) | data formatting | bytes 262144

commit v3 on v2

--- a/solution.py
+++ b/solution.py
@@ -11,23 +11,21 @@
 F32, BF16 = jnp.float32, jnp.bfloat16
 LANES, SUBS = 128, 8
 
-SIN_COEFFS = (1.0, -1.0 / 6, 1.0 / 120, -1.0 / 5040, 1.0 / 362880, -1.0 / 39916800)
-COS_COEFFS = (1.0, -1.0 / 2, 1.0 / 24, -1.0 / 720, 1.0 / 40320, -1.0 / 3628800, 1.0 / 479001600)
+SIN_COEFFS = (0.999999996, -0.041666645, 0.000520815696, -3.09516959e-06, 1.01767836e-08)
+COS_COEFFS = (0.999999953, -0.124999763, 0.00260397403, -2.1646421e-05, 9.04459312e-08)
 
 
 def horner(coeffs, x):
-    total = jnp.full_like(x, coeffs[-1])
-    for coeff in coeffs[-2::-1]:
+    total = x * coeffs[-1] + coeffs[-2]
+    for coeff in coeffs[-3::-1]:
         total = total * x + coeff
     return total
 
 
 def sin_cos(angle):
-    half = angle * 0.5
-    square = half * half
-    sine = half * horner(SIN_COEFFS, square)
-    cosine = horner(COS_COEFFS, square)
-    return 2.0 * sine * cosine, 1.0 - 2.0 * sine * sine
+    square = angle * angle
+    twice_sine = angle * horner(SIN_COEFFS, square)
+    return twice_sine * horner(COS_COEFFS, square), 1.0 - 0.5 * twice_sine * twice_sine
 
 
 def iota(shape, axis):
@@ -54,7 +52,7 @@
     grp_size, ang_size, unroll,
     children_h, present_h, interp_h, phase_h, trans_h, sources_h, trans_ids_h, list_len_h,
     out,
-    child_v, present, interp, phase, trans, sources, trans_ids, list_len, slabs, lhs, send, recv, picked, patterns, turned,
+    child_v, present, interp, phase, trans, sources, trans_ids, list_len, slabs, lhs, send, recv, picked, turned,
     load_sems, send_sem, recv_sem,
 ):
     my_grp, my_ang = lax.axis_index("grp"), lax.axis_index("ang")
@@ -217,19 +215,14 @@
 
     pltpu.make_async_copy(recv, recv, recv_sem).wait()
 
-    def widen(source, carry):
-        patterns[source] = recv[source].astype(F32)
-        return carry
-
-    lax.fori_loop(0, devices, widen, 0, unroll=8)
-
     def receive(cluster, carry):
         real = imag = jnp.zeros((SUBS, LANES), F32)
         for slot in range(slots):
             source = sources[slot, cluster]
             row = cluster * slots + slot
             op_re, op_im = picked[row, 0], picked[row, 1]
-            src_re, src_im = patterns[source, 0:SUBS], patterns[source, SUBS:2 * SUBS]
+            both = recv[source].astype(F32)
+            src_re, src_im = both[0:SUBS], both[SUBS:2 * SUBS]
             real += op_re * src_re - op_im * src_im
             imag += op_re * src_im + op_im * src_re
         for part, value in enumerate((real, imag)):
@@ -238,7 +231,7 @@
                 out[part, cluster, 4 * pol:4 * pol + 4, :] = turned[cluster, part, pl.ds(pol, 4, stride=2), :]
         return carry
 
-    lax.fori_loop(0, clusters, receive, 0, unroll=2)
+    lax.fori_loop(0, clusters, receive, 0, unroll=4)
 
     sent = recv.at[pl.ds(0, devices - 1)]
     pltpu.make_async_copy(sent, sent, send_sem).wait()
@@ -257,6 +250,7 @@
     trans = trans.transpose(0, 2, 1, 3).reshape(operators, quarters * parts, LANES)
     operands = (children, present, interp, phase, trans, sources.T, trans_ids.T, list_len)
     tile_rows = 2 * SUBS
+    operands = tuple(pltpu.with_memory_space_constraint(operand, pltpu.HBM) for operand in operands)
     received = pl.pallas_call(
         functools.partial(kernel, grp_size, ang_size, 4),
         out_shape=jax.ShapeDtypeStruct((parts, clusters, SUBS, LANES), F32),
@@ -272,14 +266,13 @@
             pltpu.VMEM((ang_size, tile_rows, LANES), BF16),
             pltpu.VMEM((devices, tile_rows, LANES), BF16),
             pltpu.VMEM((clusters * slots, 2, SUBS, LANES), F32),
-            pltpu.VMEM((devices, tile_rows, LANES), F32),
             pltpu.VMEM((clusters, 2, SUBS, LANES), F32),
             pltpu.SemaphoreType.DMA((len(operands),)),
             pltpu.SemaphoreType.DMA,
             pltpu.SemaphoreType.DMA,
         ],
         compiler_params=pltpu.CompilerParams(
-            collective_id=0, has_side_effects=True, vmem_limit_bytes=60 * 1024 * 1024
+            collective_id=0, has_side_effects=True, vmem_limit_bytes=48 * 1024 * 1024
         ),
     )(*operands)
     return received.reshape(parts, clusters, pols, angles, width)

time: 13.5 us -> 11.9 us (0.88)
  local copies, waits for them, and re-layouts: 1.57 us -> 0.66 us
  Pallas kernels: 11.8 us -> 11.1 us
    unnamed x1, local copies, waits for them, and re-layouts: 1.57 us -> 0.66 us
    pallas_call x1, Pallas kernels: 11.8 us -> 11.1 us  [local(): pl.pallas_call(functools.partial(kernel, grp_size, ang_size, 4), out_shap...]
where the time goes in v3:
time: 11.9 us; the launch traced here: 11.8 us
  Pallas kernels  11.1 us (93%)
  local copies, waits for them, and re-layouts  0.66 us (6%)
    pallas_call x1, Pallas kernels, local(): pl.pallas_call(functools.partial(kernel, grp_size, ang_size, 4), out_shap...  11.1 us
    unnamed x1, local copies, waits for them, and re-layouts  0.66 us

profile of v3, /device:TPU:0, one launch (start us, length us, event | category | flops | bytes accessed | tf_op | source)
XLA Modules:
  0.0 11.8 jit_solution(8604780784891250521)
XLA Ops:
  0.0 11.1 %shard_map.82 = f32[2,16,8,128]{3,2,1,0:T(8,128)S(1)} custom-call(bf16[16,2,2048]{2,1,0:T(2,128)(2,1)} %bitcast.13, s32[1,8]{1,0:T(1,128)} %present_h.1, f32[8,8192]{1,0:T(8,128)} %interp_h.1, f32[8,8192]{1,0:T(8,128)} %phase_h.1, f32[316,8,128]{2,1,0:T(8,128)} %bitcast.12, s32[8,16]{1,0:T(8,128)} %bitcast.14, s32[8,16]{1,0:T(8,128)} %bitcast.15, s32[16]{0:T(128)} %list_len_h.1), custom_call_target="tpu_custom_call" | custom-call | tf_op jit(solution)/shard_map/pallas_call | solution.py:254
  11.1 0.7 %copy.12 = f32[2,16,2,1,512]{4,3,2,1,0:T(1,128)} copy(f32[2,16,2,1,512]{4,3,2,1,0:T(1,128)S(1)} %bitcast.11) | data formatting | bytes 262144

commit v4 on v3

--- a/solution.py
+++ b/solution.py
@@ -10,6 +10,7 @@
 MESH = pl.DeviceIdType.MESH
 F32, BF16 = jnp.float32, jnp.bfloat16
 LANES, SUBS = 128, 8
+UNROLL = 2
 
 SIN_COEFFS = (0.999999996, -0.041666645, 0.000520815696, -3.09516959e-06, 1.01767836e-08)
 COS_COEFFS = (0.999999953, -0.124999763, 0.00260397403, -2.1646421e-05, 9.04459312e-08)
@@ -52,7 +53,8 @@
     grp_size, ang_size, unroll,
     children_h, present_h, interp_h, phase_h, trans_h, sources_h, trans_ids_h, list_len_h,
     out,
-    child_v, present, interp, phase, trans, sources, trans_ids, list_len, slabs, lhs, send, recv, picked, turned,
+    child_v, present, interp, phase, trans, sources, trans_ids, list_len, slabs, lhs,
+    stage_a, stage_b, send, recv, picked, turned,
     load_sems, send_sem, recv_sem,
 ):
     my_grp, my_ang = lax.axis_index("grp"), lax.axis_index("ang")
@@ -86,11 +88,11 @@
     for octant in range(octants):
         mask = jnp.where(sub == octant, present[0, octant].astype(F32), mask)
 
-    coarse_tiles = slabs.shape[0]
-    for tile in range(coarse_tiles):
-        part = child_v[:, :, tile * LANES:(tile + 1) * LANES].astype(F32)
-        for row in range(part.shape[0]):
-            slabs[tile, 2 * row:2 * row + 2, :] = part[row]
+    chunks = child_v.shape[0] // (2 * octants)
+    chunk_tiles = child_v.shape[1] // 2
+    coarse_tiles = chunks * chunk_tiles
+    for row in range(child_v.shape[0]):
+        slabs[row * 2 * chunk_tiles:(row + 1) * 2 * chunk_tiles, :] = child_v[row].astype(F32)
     half_width = interp.shape[0] // 2
     lane = iota((SUBS, LANES), 1)
 
@@ -101,7 +103,15 @@
         groups = []
         for reim in range(2):
             tiles = [
-                slabs[tile, pl.ds(2 * octants * reim + pol, octants, stride=2), :] * mask
+                slabs[
+                    pl.ds(
+                        2 * chunk_tiles * (octants * chunks * reim + tile // chunk_tiles)
+                        + 2 * (tile % chunk_tiles) + pol,
+                        octants,
+                        stride=2 * chunk_tiles * chunks,
+                    ),
+                    :,
+                ] * mask
                 for tile in range(coarse_tiles)
             ]
             groups.append(tiles)
@@ -132,8 +142,7 @@
     def blank(rows):
         return jnp.zeros((rows, LANES), BF16)
 
-    def one_block(block):
-        real, imag = [], []
+    def refine(block, stage):
         for half in range(2):
             x = lhs[block, half]
             cols = []
@@ -144,59 +153,64 @@
                     pieces += [blank(32 * tile), piece] if tile else [piece]
                     pieces.append(blank(LANES - band_rows - 32 * tile))
                 cols.append(jnp.concatenate(pieces, axis=0))
-            fine = jnp.dot(
+            stage[half] = jnp.dot(
                 jnp.concatenate([x, x], axis=1), jnp.concatenate(cols, axis=1), preferred_element_type=F32
             )
+
+    def combine(block, stage):
+        real, imag = [], []
+        for half in range(2):
             for tile in range(2):
                 at = pl.multiple_of((4 * block + 2 * half + tile) * LANES, LANES)
                 sine, cosine = sin_cos(phase[:, pl.ds(at, LANES)])
+                cols = pl.ds(tile * LANES, LANES)
                 for pol in range(2):
-                    re = fine[16 * pol:16 * pol + 8, tile * LANES:(tile + 1) * LANES]
-                    im = fine[16 * pol + 8:16 * pol + 16, tile * LANES:(tile + 1) * LANES]
+                    re = stage[half, 16 * pol:16 * pol + 8, cols]
+                    im = stage[half, 16 * pol + 8:16 * pol + 16, cols]
                     real.append(re * cosine - im * sine)
                     imag.append(re * sine + im * cosine)
-        return jnp.concatenate([sublane_sums(real, sub), sublane_sums(imag, sub)], axis=0).astype(BF16)
-
-    def post(block):
+        send[block] = jnp.concatenate(
+            [sublane_sums(real, sub), sublane_sums(imag, sub)], axis=0
+        ).astype(BF16)
+
+    def post(block, own):
         for step in range(grp_size):
-            grp = lax.rem(my_grp + step, grp_size)
-
-            def away():
-                pltpu.make_async_remote_copy(
-                    src_ref=send.at[block], dst_ref=recv.at[me], send_sem=send_sem, recv_sem=recv_sem,
-                    device_id=(grp, block), device_id_type=MESH,
-                ).start()
-
-            if step:
-                away()
-            else:
-                pl.when(block != my_ang)(away)
-
-                @pl.when(block == my_ang)
-                def _():
-                    pltpu.make_async_copy(send.at[block], recv.at[me], recv_sem).start()
-
-    def blocks_of(step):
-        return [lax.rem(my_ang + 1 + step * unroll + i, ang_size) for i in range(unroll)]
-
-    def aggregate(step):
-        for block in blocks_of(step):
-            send[block] = one_block(block)
-
-    def dispatch(step):
-        for block in blocks_of(step):
-            post(block)
-
-    aggregate(0)
+            if own and not step:
+                pltpu.make_async_copy(send.at[block], recv.at[me], recv_sem).start()
+                continue
+            pltpu.make_async_remote_copy(
+                src_ref=send.at[block], dst_ref=recv.at[me], send_sem=send_sem, recv_sem=recv_sem,
+                device_id=(lax.rem(my_grp + step, grp_size), block), device_id_type=MESH,
+            ).start()
+
+    def block_at(step):
+        return lax.rem(my_ang + 1 + step, ang_size)
+
+    def refine_group(group, stages):
+        for i in range(unroll):
+            refine(block_at(group * unroll + i), stages.at[i])
+
+    def combine_group(group, stages, last=False):
+        for i in range(unroll):
+            combine(block_at(group * unroll + i), stages.at[i])
+        for i in range(unroll):
+            post(block_at(group * unroll + i), last and i == unroll - 1)
+
+    refine_group(0, stage_a)
     pl.semaphore_wait(barrier, devices - 1)
-    dispatch(0)
+    rounds = ang_size // (2 * unroll)
 
     def advance(step, carry):
-        aggregate(step)
-        dispatch(step)
+        refine_group(2 * step + 1, stage_b)
+        combine_group(2 * step, stage_a)
+        refine_group(2 * step + 2, stage_a)
+        combine_group(2 * step + 1, stage_b)
         return carry
 
-    lax.fori_loop(1, ang_size // unroll, advance, 0)
+    lax.fori_loop(0, rounds - 1, advance, 0)
+    refine_group(2 * rounds - 1, stage_b)
+    combine_group(2 * rounds - 2, stage_a)
+    combine_group(2 * rounds - 1, stage_b, last=True)
 
     for load in loads[4:]:
         load.wait()
@@ -241,18 +255,21 @@
     parts, own, octants, pols, angles, coarse = children.shape
     operators, width = trans.shape[1:]
     clusters, slots = sources.shape
+    assert ang_size % (2 * UNROLL) == 0
     devices = grp_size * ang_size
     quarters = width // LANES
     assert (parts, own, octants, pols, angles, quarters) == (2, 1, SUBS, 2, 1, 4)
     assert interp.shape[0] == SUBS and interp.shape[1] == ang_size * width == 4 * coarse
-    children = children.reshape(parts * octants, pols, coarse)
+    chunk = SUBS * LANES
+    children = children.reshape(parts * octants, pols, coarse // chunk, SUBS, LANES)
+    children = children.transpose(0, 2, 3, 1, 4).reshape(parts * octants * coarse // chunk, 2 * SUBS, LANES)
     trans = trans.transpose(1, 0, 2).reshape(operators, parts, quarters, LANES)
     trans = trans.transpose(0, 2, 1, 3).reshape(operators, quarters * parts, LANES)
     operands = (children, present, interp, phase, trans, sources.T, trans_ids.T, list_len)
     tile_rows = 2 * SUBS
     operands = tuple(pltpu.with_memory_space_constraint(operand, pltpu.HBM) for operand in operands)
     received = pl.pallas_call(
-        functools.partial(kernel, grp_size, ang_size, 4),
+        functools.partial(kernel, grp_size, ang_size, UNROLL),
         out_shape=jax.ShapeDtypeStruct((parts, clusters, SUBS, LANES), F32),
         in_specs=[pl.BlockSpec(memory_space=pltpu.HBM)] * len(operands),
         out_specs=pl.BlockSpec(memory_space=pltpu.VMEM),
@@ -261,8 +278,10 @@
                 (pltpu.SMEM if operand.dtype == jnp.int32 else pltpu.VMEM)(operand.shape, operand.dtype)
                 for operand in operands
             ),
-            pltpu.VMEM((coarse // LANES, parts * octants * pols, LANES), F32),
+            pltpu.VMEM((children.size // LANES, LANES), F32),
             pltpu.VMEM((coarse // LANES, 2, parts * octants * pols, LANES), BF16),
+            pltpu.VMEM((UNROLL, 2, parts * octants * pols, 2 * LANES), F32),
+            pltpu.VMEM((UNROLL, 2, parts * octants * pols, 2 * LANES), F32),
             pltpu.VMEM((ang_size, tile_rows, LANES), BF16),
             pltpu.VMEM((devices, tile_rows, LANES), BF16),
             pltpu.VMEM((clusters * slots, 2, SUBS, LANES), F32),

time: 11.9 us -> 12.5 us (1.050)
  Pallas kernels: 11.1 us -> 11.7 us
    pallas_call x1, Pallas kernels: 11.1 us -> 11.7 us  [local(): pl.pallas_call(functools.partial(kernel, grp_size, ang_size, UNROLL), out...]
where the time goes in v4:
time: 12.5 us; the launch traced here: 12.3 us
  Pallas kernels  11.7 us (94%)
  local copies, waits for them, and re-layouts  0.66 us (5%)
    pallas_call x1, Pallas kernels, local(): pl.pallas_call(functools.partial(kernel, grp_size, ang_size, UNROLL), out...  11.7 us
    unnamed x1, local copies, waits for them, and re-layouts  0.66 us

profile of v4, /device:TPU:0, one launch (start us, length us, event | category | flops | bytes accessed | tf_op | source)
XLA Modules:
  0.0 12.3 jit_solution(91613225460980800)
XLA Ops:
  0.0 11.7 %shard_map.82 = f32[2,16,8,128]{3,2,1,0:T(8,128)S(1)} custom-call(bf16[32,16,128]{2,1,0:T(8,128)(2,1)} %bitcast.17, s32[1,8]{1,0:T(1,128)} %present_h.1, f32[8,8192]{1,0:T(8,128)} %interp_h.1, f32[8,8192]{1,0:T(8,128)} %phase_h.1, f32[316,8,128]{2,1,0:T(8,128)} %bitcast.16, s32[8,16]{1,0:T(8,128)} %bitcast.18, s32[8,16]{1,0:T(8,128)} %bitcast.19, s32[16]{0:T(128)} %list_len_h.1), custom_call_target="tpu_custom_call" | custom-call | tf_op jit(solution)/shard_map/pallas_call | solution.py:271
  11.7 0.7 %copy.13 = f32[2,16,2,1,512]{4,3,2,1,0:T(1,128)} copy(f32[2,16,2,1,512]{4,3,2,1,0:T(1,128)S(1)} %bitcast.15) | data formatting | bytes 262144

commit v5 on v4

--- a/solution.py
+++ b/solution.py
@@ -10,7 +10,7 @@
 MESH = pl.DeviceIdType.MESH
 F32, BF16 = jnp.float32, jnp.bfloat16
 LANES, SUBS = 128, 8
-UNROLL = 2
+UNROLL = 4
 
 SIN_COEFFS = (0.999999996, -0.041666645, 0.000520815696, -3.09516959e-06, 1.01767836e-08)
 COS_COEFFS = (0.999999953, -0.124999763, 0.00260397403, -2.1646421e-05, 9.04459312e-08)
@@ -61,6 +61,15 @@
     devices = grp_size * ang_size
     me = my_grp * ang_size + my_ang
 
+    def wrap(index, size):
+        return jnp.where(index >= size, index - size, index)
+
+    def grp_at(step):
+        return wrap(my_grp + step, grp_size)
+
+    def ang_at(step):
+        return wrap(my_ang + step, ang_size)
+
     pairs = (
         (children_h, child_v), (present_h, present), (interp_h, interp), (phase_h, phase),
         (trans_h, trans), (sources_h, sources), (trans_ids_h, trans_ids), (list_len_h, list_len),
@@ -71,14 +80,12 @@
 
     barrier = pltpu.get_barrier_semaphore()
 
-    def greet(step, carry):
-        other = lax.rem(me + step, devices)
-        pl.semaphore_signal(
-            barrier, inc=1, device_id=(other // ang_size, lax.rem(other, ang_size)), device_id_type=MESH
-        )
-        return carry
-
-    lax.fori_loop(1, devices, greet, 0)
+    for grp_step in range(grp_size):
+        for ang_step in range(ang_size):
+            if grp_step or ang_step:
+                pl.semaphore_signal(
+                    barrier, inc=1, device_id=(grp_at(grp_step), ang_at(ang_step)), device_id_type=MESH
+                )
 
     loads[0].wait()
     loads[1].wait()
@@ -180,37 +187,46 @@
                 continue
             pltpu.make_async_remote_copy(
                 src_ref=send.at[block], dst_ref=recv.at[me], send_sem=send_sem, recv_sem=recv_sem,
-                device_id=(lax.rem(my_grp + step, grp_size), block), device_id_type=MESH,
+                device_id=(grp_at(step), block), device_id_type=MESH,
             ).start()
 
     def block_at(step):
-        return lax.rem(my_ang + 1 + step, ang_size)
+        return ang_at(1 + step)
 
     def refine_group(group, stages):
         for i in range(unroll):
             refine(block_at(group * unroll + i), stages.at[i])
 
-    def combine_group(group, stages, last=False):
+    def combine_group(group, stages):
         for i in range(unroll):
             combine(block_at(group * unroll + i), stages.at[i])
+
+    def post_group(group, last=False):
         for i in range(unroll):
             post(block_at(group * unroll + i), last and i == unroll - 1)
 
-    refine_group(0, stage_a)
-    pl.semaphore_wait(barrier, devices - 1)
-    rounds = ang_size // (2 * unroll)
-
-    def advance(step, carry):
+    def one_round(step, last=False):
         refine_group(2 * step + 1, stage_b)
         combine_group(2 * step, stage_a)
-        refine_group(2 * step + 2, stage_a)
+        if isinstance(step, int) and step == 0:
+            pl.semaphore_wait(barrier, devices - 1)
+        post_group(2 * step)
+        if not last:
+            refine_group(2 * step + 2, stage_a)
         combine_group(2 * step + 1, stage_b)
+        post_group(2 * step + 1, last)
+
+    def advance(step, carry):
+        one_round(step)
         return carry
 
-    lax.fori_loop(0, rounds - 1, advance, 0)
-    refine_group(2 * rounds - 1, stage_b)
-    combine_group(2 * rounds - 2, stage_a)
-    combine_group(2 * rounds - 1, stage_b, last=True)
+    refine_group(0, stage_a)
+    rounds = ang_size // (2 * unroll)
+    one_round(0, rounds == 1)
+    if rounds > 2:
+        lax.fori_loop(1, rounds - 1, advance, 0)
+    if rounds > 1:
+        one_round(rounds - 1, True)
 
     for load in loads[4:]:
         load.wait()

time: 12.5 us -> 11.5 us (0.920)
  the two profiles are of different devices: /device:TPU:0 before, /device:TPU:1 now
where the time goes in v5:
time: 11.5 us; the launch traced here: 11.4 us
  Pallas kernels  10.7 us (93%)
  local copies, waits for them, and re-layouts  0.66 us (6%)
    pallas_call x1, Pallas kernels, local(): pl.pallas_call(functools.partial(kernel, grp_size, ang_size, UNROLL), out...  10.7 us
    unnamed x1, local copies, waits for them, and re-layouts  0.66 us

profile of v5, /device:TPU:1, one launch (start us, length us, event | category | flops | bytes accessed | tf_op | source)
XLA Modules:
  0.0 11.4 jit_solution(14233181061260079486)
XLA Ops:
  0.0 10.7 %shard_map.82 = f32[2,16,8,128]{3,2,1,0:T(8,128)S(1)} custom-call(bf16[32,16,128]{2,1,0:T(8,128)(2,1)} %bitcast.17, s32[1,8]{1,0:T(1,128)} %present_h.1, f32[8,8192]{1,0:T(8,128)} %interp_h.1, f32[8,8192]{1,0:T(8,128)} %phase_h.1, f32[316,8,128]{2,1,0:T(8,128)} %bitcast.16, s32[8,16]{1,0:T(8,128)} %bitcast.18, s32[8,16]{1,0:T(8,128)} %bitcast.19, s32[16]{0:T(128)} %list_len_h.1), custom_call_target="tpu_custom_call" | custom-call | tf_op jit(solution)/shard_map/pallas_call | solution.py:287
  10.7 0.7 %copy.13 = f32[2,16,2,1,512]{4,3,2,1,0:T(1,128)} copy(f32[2,16,2,1,512]{4,3,2,1,0:T(1,128)S(1)} %bitcast.15) | data formatting | bytes 262144

commit v6 on v5

--- a/solution.py
+++ b/solution.py
@@ -191,7 +191,12 @@
             ).start()
 
     def block_at(step):
-        return ang_at(1 + step)
+        code = ang_size - 1 - step
+        weight, block = 1, 0
+        while weight < ang_size:
+            digit = lax.rem(code // weight + lax.div(my_ang, weight), 2)
+            block, weight = block + digit * weight, 2 * weight
+        return block
 
     def refine_group(group, stages):
         for i in range(unroll):
@@ -271,7 +276,7 @@
     parts, own, octants, pols, angles, coarse = children.shape
     operators, width = trans.shape[1:]
     clusters, slots = sources.shape
-    assert ang_size % (2 * UNROLL) == 0
+    assert ang_size % (2 * UNROLL) == 0 and ang_size & (ang_size - 1) == 0
     devices = grp_size * ang_size
     quarters = width // LANES
     assert (parts, own, octants, pols, angles, quarters) == (2, 1, SUBS, 2, 1, 4)

time: 11.5 us -> 12.6 us (1.096)
  the two profiles are of different devices: /device:TPU:1 before, /device:TPU:0 now
where the time goes in v6:
time: 12.6 us; the launch traced here: 12.5 us
  Pallas kernels  11.8 us (94%)
  local copies, waits for them, and re-layouts  0.66 us (5%)
    pallas_call x1, Pallas kernels, local(): pl.pallas_call(functools.partial(kernel, grp_size, ang_size, UNROLL), out...  11.8 us
    unnamed x1, local copies, waits for them, and re-layouts  0.66 us

profile of v6, /device:TPU:0, one launch (start us, length us, event | category | flops | bytes accessed | tf_op | source)
XLA Modules:
  0.0 12.5 jit_solution(5017838197877257288)
XLA Ops:
  0.0 11.8 %shard_map.82 = f32[2,16,8,128]{3,2,1,0:T(8,128)S(1)} custom-call(bf16[32,16,128]{2,1,0:T(8,128)(2,1)} %bitcast.17, s32[1,8]{1,0:T(1,128)} %present_h.1, f32[8,8192]{1,0:T(8,128)} %interp_h.1, f32[8,8192]{1,0:T(8,128)} %phase_h.1, f32[316,8,128]{2,1,0:T(8,128)} %bitcast.16, s32[8,16]{1,0:T(8,128)} %bitcast.18, s32[8,16]{1,0:T(8,128)} %bitcast.19, s32[16]{0:T(128)} %list_len_h.1), custom_call_target="tpu_custom_call" | custom-call | tf_op jit(solution)/shard_map/pallas_call | solution.py:292
  11.8 0.7 %copy.13 = f32[2,16,2,1,512]{4,3,2,1,0:T(1,128)} copy(f32[2,16,2,1,512]{4,3,2,1,0:T(1,128)S(1)} %bitcast.15) | data formatting | bytes 262144

commit v7 on v5

--- a/solution.py
+++ b/solution.py
@@ -55,7 +55,7 @@
     out,
     child_v, present, interp, phase, trans, sources, trans_ids, list_len, slabs, lhs,
     stage_a, stage_b, send, recv, picked, turned,
-    load_sems, send_sem, recv_sem,
+    load_sems, send_sem, recv_sems, forward_sems,
 ):
     my_grp, my_ang = lax.axis_index("grp"), lax.axis_index("ang")
     devices = grp_size * ang_size
@@ -80,12 +80,10 @@
 
     barrier = pltpu.get_barrier_semaphore()
 
-    for grp_step in range(grp_size):
-        for ang_step in range(ang_size):
-            if grp_step or ang_step:
-                pl.semaphore_signal(
-                    barrier, inc=1, device_id=(grp_at(grp_step), ang_at(ang_step)), device_id_type=MESH
-                )
+    for step in range(1, ang_size):
+        pl.semaphore_signal(barrier, inc=1, device_id=(my_grp, ang_at(step)), device_id_type=MESH)
+    for step in range(1, grp_size):
+        pl.semaphore_signal(barrier, inc=1, device_id=(grp_at(step), my_ang), device_id_type=MESH)
 
     loads[0].wait()
     loads[1].wait()
@@ -180,14 +178,28 @@
             [sublane_sums(real, sub), sublane_sums(imag, sub)], axis=0
         ).astype(BF16)
 
-    def post(block, own):
-        for step in range(grp_size):
-            if own and not step:
-                pltpu.make_async_copy(send.at[block], recv.at[me], recv_sem).start()
-                continue
+    def post(step, own):
+        block = block_at(step)
+        src, dst = send.at[block], recv.at[my_grp * ang_size + step]
+        arrived = recv_sems.at[step // unroll]
+        if own:
+            pltpu.make_async_copy(src, dst, arrived).start()
+        else:
             pltpu.make_async_remote_copy(
-                src_ref=send.at[block], dst_ref=recv.at[me], send_sem=send_sem, recv_sem=recv_sem,
-                device_id=(grp_at(step), block), device_id_type=MESH,
+                src_ref=src, dst_ref=dst, send_sem=send_sem, recv_sem=arrived,
+                device_id=(my_grp, block), device_id_type=MESH,
+            ).start()
+
+    def chunk_of(grp, group):
+        return recv.at[pl.ds(grp * ang_size + group * unroll, unroll)]
+
+    def forward(group):
+        chunk = chunk_of(my_grp, group)
+        pltpu.make_async_copy(chunk, chunk, recv_sems.at[group]).wait()
+        for step in range(1, grp_size):
+            pltpu.make_async_remote_copy(
+                src_ref=chunk, dst_ref=chunk, send_sem=send_sem, recv_sem=forward_sems.at[step - 1, group],
+                device_id=(grp_at(step), my_ang), device_id_type=MESH,
             ).start()
 
     def block_at(step):
@@ -203,18 +215,22 @@
 
     def post_group(group, last=False):
         for i in range(unroll):
-            post(block_at(group * unroll + i), last and i == unroll - 1)
+            post(group * unroll + i, last and i == unroll - 1)
 
     def one_round(step, last=False):
         refine_group(2 * step + 1, stage_b)
         combine_group(2 * step, stage_a)
         if isinstance(step, int) and step == 0:
-            pl.semaphore_wait(barrier, devices - 1)
+            pl.semaphore_wait(barrier, ang_size + grp_size - 2)
         post_group(2 * step)
+        if not (isinstance(step, int) and step == 0):
+            forward(2 * step - 2)
         if not last:
             refine_group(2 * step + 2, stage_a)
         combine_group(2 * step + 1, stage_b)
         post_group(2 * step + 1, last)
+        if not (isinstance(step, int) and step == 0):
+            forward(2 * step - 1)
 
     def advance(step, carry):
         one_round(step)
@@ -227,6 +243,8 @@
         lax.fori_loop(1, rounds - 1, advance, 0)
     if rounds > 1:
         one_round(rounds - 1, True)
+    for group in range(2 * rounds - 2, 2 * rounds):
+        forward(group)
 
     for load in loads[4:]:
         load.wait()
@@ -235,6 +253,11 @@
 
     def pick(cluster, carry):
         for slot in range(slots):
+            source = sources[slot, cluster]
+            source_grp = lax.div(source, ang_size)
+            came = my_ang - 1 - (source - source_grp * ang_size)
+            came = jnp.where(came < 0, came + ang_size, came)
+            sources[slot, cluster] = source_grp * ang_size + came
             both = trans[trans_ids[slot, cluster]]
             both = both * jnp.where(slot < list_len[cluster], 1.0, 0.0)
             picked[cluster * slots + slot, 0] = jnp.where(even, both, pltpu.roll(both, 1, 0))
@@ -243,15 +266,17 @@
 
     lax.fori_loop(0, clusters, pick, 0, unroll=2)
 
-    pltpu.make_async_copy(recv, recv, recv_sem).wait()
+    for step in range(1, grp_size):
+        for group in range(2 * rounds):
+            chunk = chunk_of(wrap(my_grp + grp_size - step, grp_size), group)
+            pltpu.make_async_copy(chunk, chunk, forward_sems.at[step - 1, group]).wait()
 
     def receive(cluster, carry):
         real = imag = jnp.zeros((SUBS, LANES), F32)
         for slot in range(slots):
-            source = sources[slot, cluster]
             row = cluster * slots + slot
             op_re, op_im = picked[row, 0], picked[row, 1]
-            both = recv[source].astype(F32)
+            both = recv[sources[slot, cluster]].astype(F32)
             src_re, src_im = both[0:SUBS], both[SUBS:2 * SUBS]
             real += op_re * src_re - op_im * src_im
             imag += op_re * src_im + op_im * src_re
@@ -304,7 +329,8 @@
             pltpu.VMEM((clusters, 2, SUBS, LANES), F32),
             pltpu.SemaphoreType.DMA((len(operands),)),
             pltpu.SemaphoreType.DMA,
-            pltpu.SemaphoreType.DMA,
+            pltpu.SemaphoreType.DMA((ang_size // UNROLL,)),
+            pltpu.SemaphoreType.DMA((max(grp_size - 1, 1), ang_size // UNROLL)),
         ],
         compiler_params=pltpu.CompilerParams(
             collective_id=0, has_side_effects=True, vmem_limit_bytes=48 * 1024 * 1024

time: 11.5 us -> 15.9 us (1.38)
  the two profiles are of different devices: /device:TPU:1 before, /device:TPU:0 now
where the time goes in v7:
time: 15.9 us; the launch traced here: 15.8 us
  Pallas kernels  15.1 us (95%)
  local copies, waits for them, and re-layouts  0.66 us (4%)
    pallas_call x1, Pallas kernels, local(): pl.pallas_call(functools.partial(kernel, grp_size, ang_size, UNROLL), out...  15.1 us
    unnamed x1, local copies, waits for them, and re-layouts  0.66 us

profile of v7, /device:TPU:0, one launch (start us, length us, event | category | flops | bytes accessed | tf_op | source)
XLA Modules:
  0.0 15.8 jit_solution(11002112747966825003)
XLA Ops:
  0.0 15.1 %shard_map.82 = f32[2,16,8,128]{3,2,1,0:T(8,128)S(1)} custom-call(bf16[32,16,128]{2,1,0:T(8,128)(2,1)} %bitcast.17, s32[1,8]{1,0:T(1,128)} %present_h.1, f32[8,8192]{1,0:T(8,128)} %interp_h.1, f32[8,8192]{1,0:T(8,128)} %phase_h.1, f32[316,8,128]{2,1,0:T(8,128)} %bitcast.16, s32[8,16]{1,0:T(8,128)} %bitcast.18, s32[8,16]{1,0:T(8,128)} %bitcast.19, s32[16]{0:T(128)} %list_len_h.1), custom_call_target="tpu_custom_call" | custom-call | tf_op jit(solution)/shard_map/pallas_call | solution.py:312
  15.1 0.7 %copy.13 = f32[2,16,2,1,512]{4,3,2,1,0:T(1,128)} copy(f32[2,16,2,1,512]{4,3,2,1,0:T(1,128)S(1)} %bitcast.15) | data formatting | bytes 262144

commit v8 on v5

--- a/solution.py
+++ b/solution.py
@@ -54,7 +54,7 @@
     children_h, present_h, interp_h, phase_h, trans_h, sources_h, trans_ids_h, list_len_h,
     out,
     child_v, present, interp, phase, trans, sources, trans_ids, list_len, slabs, lhs,
-    stage_a, stage_b, send, recv, picked, turned,
+    stage, send, recv, picked, turned,
     load_sems, send_sem, recv_sem,
 ):
     my_grp, my_ang = lax.axis_index("grp"), lax.axis_index("ang")
@@ -75,7 +75,7 @@
         (trans_h, trans), (sources_h, sources), (trans_ids_h, trans_ids), (list_len_h, list_len),
     )
     loads = [pltpu.make_async_copy(src, dst, load_sems.at[i]) for i, (src, dst) in enumerate(pairs)]
-    for load in loads:
+    for load in loads[:4]:
         load.start()
 
     barrier = pltpu.get_barrier_semaphore()
@@ -133,6 +133,8 @@
 
     loads[2].wait()
     loads[3].wait()
+    for load in loads[4:]:
+        load.start()
 
     band_rows = 48
     gap = iota((band_rows, LANES), 0) - iota((band_rows, LANES), 1) // 4
@@ -205,28 +207,23 @@
         for i in range(unroll):
             post(block_at(group * unroll + i), last and i == unroll - 1)
 
-    def one_round(step, last=False):
-        refine_group(2 * step + 1, stage_b)
-        combine_group(2 * step, stage_a)
-        if isinstance(step, int) and step == 0:
+    def one_group(group, last=False):
+        refine_group(group, stage)
+        combine_group(group, stage)
+        if isinstance(group, int) and group == 0:
             pl.semaphore_wait(barrier, devices - 1)
-        post_group(2 * step)
-        if not last:
-            refine_group(2 * step + 2, stage_a)
-        combine_group(2 * step + 1, stage_b)
-        post_group(2 * step + 1, last)
-
-    def advance(step, carry):
-        one_round(step)
+        post_group(group, last)
+
+    def advance(group, carry):
+        one_group(group)
         return carry
 
-    refine_group(0, stage_a)
-    rounds = ang_size // (2 * unroll)
-    one_round(0, rounds == 1)
-    if rounds > 2:
-        lax.fori_loop(1, rounds - 1, advance, 0)
-    if rounds > 1:
-        one_round(rounds - 1, True)
+    groups = ang_size // unroll
+    one_group(0, groups == 1)
+    if groups > 2:
+        lax.fori_loop(1, groups - 1, advance, 0)
+    if groups > 1:
+        one_group(groups - 1, True)
 
     for load in loads[4:]:
         load.wait()
@@ -271,7 +268,7 @@
     parts, own, octants, pols, angles, coarse = children.shape
     operators, width = trans.shape[1:]
     clusters, slots = sources.shape
-    assert ang_size % (2 * UNROLL) == 0
+    assert ang_size % UNROLL == 0
     devices = grp_size * ang_size
     quarters = width // LANES
     assert (parts, own, octants, pols, angles, quarters) == (2, 1, SUBS, 2, 1, 4)
@@ -297,7 +294,6 @@
             pltpu.VMEM((children.size // LANES, LANES), F32),
             pltpu.VMEM((coarse // LANES, 2, parts * octants * pols, LANES), BF16),
             pltpu.VMEM((UNROLL, 2, parts * octants * pols, 2 * LANES), F32),
-            pltpu.VMEM((UNROLL, 2, parts * octants * pols, 2 * LANES), F32),
             pltpu.VMEM((ang_size, tile_rows, LANES), BF16),
             pltpu.VMEM((devices, tile_rows, LANES), BF16),
             pltpu.VMEM((clusters * slots, 2, SUBS, LANES), F32),

time: 11.5 us -> 11.7 us (1.017)
  the two profiles are of different devices: /device:TPU:1 before, /device:TPU:0 now
where the time goes in v8:
time: 11.7 us; the launch traced here: 11.6 us
  Pallas kernels  10.9 us (93%)
  local copies, waits for them, and re-layouts  0.66 us (6%)
    pallas_call x1, Pallas kernels, local(): pl.pallas_call(functools.partial(kernel, grp_size, ang_size, UNROLL), out...  10.9 us
    unnamed x1, local copies, waits for them, and re-layouts  0.66 us

profile of v8, /device:TPU:0, one launch (start us, length us, event | category | flops | bytes accessed | tf_op | source)
XLA Modules:
  0.0 11.6 jit_solution(18443051261129522436)
XLA Ops:
  0.0 10.9 %shard_map.82 = f32[2,16,8,128]{3,2,1,0:T(8,128)S(1)} custom-call(bf16[32,16,128]{2,1,0:T(8,128)(2,1)} %bitcast.17, s32[1,8]{1,0:T(1,128)} %present_h.1, f32[8,8192]{1,0:T(8,128)} %interp_h.1, f32[8,8192]{1,0:T(8,128)} %phase_h.1, f32[316,8,128]{2,1,0:T(8,128)} %bitcast.16, s32[8,16]{1,0:T(8,128)} %bitcast.18, s32[8,16]{1,0:T(8,128)} %bitcast.19, s32[16]{0:T(128)} %list_len_h.1), custom_call_target="tpu_custom_call" | custom-call | tf_op jit(solution)/shard_map/pallas_call | solution.py:284
  10.9 0.7 %copy.13 = f32[2,16,2,1,512]{4,3,2,1,0:T(1,128)} copy(f32[2,16,2,1,512]{4,3,2,1,0:T(1,128)S(1)} %bitcast.15) | data formatting | bytes 262144

commit v9 on v8

--- a/solution.py
+++ b/solution.py
@@ -80,12 +80,16 @@
 
     barrier = pltpu.get_barrier_semaphore()
 
-    for grp_step in range(grp_size):
-        for ang_step in range(ang_size):
-            if grp_step or ang_step:
-                pl.semaphore_signal(
-                    barrier, inc=1, device_id=(grp_at(grp_step), ang_at(ang_step)), device_id_type=MESH
-                )
+    def greet(ang_step, carry):
+        for grp_step in range(grp_size):
+            pl.semaphore_signal(
+                barrier, inc=1, device_id=(grp_at(grp_step), ang_at(ang_step)), device_id_type=MESH
+            )
+        return carry
+
+    lax.fori_loop(1, ang_size, greet, 0)
+    for grp_step in range(1, grp_size):
+        pl.semaphore_signal(barrier, inc=1, device_id=(grp_at(grp_step), my_ang), device_id_type=MESH)
 
     loads[0].wait()
     loads[1].wait()
@@ -182,15 +186,23 @@
             [sublane_sums(real, sub), sublane_sums(imag, sub)], axis=0
         ).astype(BF16)
 
-    def post(block, own):
+    def post(block, may_be_own):
         for step in range(grp_size):
-            if own and not step:
-                pltpu.make_async_copy(send.at[block], recv.at[me], recv_sem).start()
-                continue
-            pltpu.make_async_remote_copy(
-                src_ref=send.at[block], dst_ref=recv.at[me], send_sem=send_sem, recv_sem=recv_sem,
-                device_id=(grp_at(step), block), device_id_type=MESH,
-            ).start()
+
+            def away():
+                pltpu.make_async_remote_copy(
+                    src_ref=send.at[block], dst_ref=recv.at[me], send_sem=send_sem, recv_sem=recv_sem,
+                    device_id=(grp_at(step), block), device_id_type=MESH,
+                ).start()
+
+            if step or not may_be_own:
+                away()
+            else:
+                pl.when(block != my_ang)(away)
+
+                @pl.when(block == my_ang)
+                def _():
+                    pltpu.make_async_copy(send.at[block], recv.at[me], recv_sem).start()
 
     def block_at(step):
         return ang_at(1 + step)
@@ -203,27 +215,22 @@
         for i in range(unroll):
             combine(block_at(group * unroll + i), stages.at[i])
 
-    def post_group(group, last=False):
+    def post_group(group):
         for i in range(unroll):
-            post(block_at(group * unroll + i), last and i == unroll - 1)
-
-    def one_group(group, last=False):
+            post(block_at(group * unroll + i), i == unroll - 1)
+
+    def one_group(group, carry):
         refine_group(group, stage)
         combine_group(group, stage)
-        if isinstance(group, int) and group == 0:
+
+        @pl.when(group == 0)
+        def _():
             pl.semaphore_wait(barrier, devices - 1)
-        post_group(group, last)
-
-    def advance(group, carry):
-        one_group(group)
+
+        post_group(group)
         return carry
 
-    groups = ang_size // unroll
-    one_group(0, groups == 1)
-    if groups > 2:
-        lax.fori_loop(1, groups - 1, advance, 0)
-    if groups > 1:
-        one_group(groups - 1, True)
+    lax.fori_loop(0, ang_size // unroll, one_group, 0)
 
     for load in loads[4:]:
         load.wait()

time: 11.7 us -> 11.7 us (level)
  no operation moved by 1% of the time
where the time goes in v9:
time: 11.7 us; the launch traced here: 11.6 us
  Pallas kernels  10.9 us (93%)
  local copies, waits for them, and re-layouts  0.66 us (6%)
    pallas_call x1, Pallas kernels, local(): pl.pallas_call(functools.partial(kernel, grp_size, ang_size, UNROLL), out...  10.9 us
    unnamed x1, local copies, waits for them, and re-layouts  0.66 us

profile of v9, /device:TPU:0, one launch (start us, length us, event | category | flops | bytes accessed | tf_op | source)
XLA Modules:
  0.0 11.6 jit_solution(12432085551810849468)
XLA Ops:
  0.0 10.9 %shard_map.82 = f32[2,16,8,128]{3,2,1,0:T(8,128)S(1)} custom-call(bf16[32,16,128]{2,1,0:T(8,128)(2,1)} %bitcast.17, s32[1,8]{1,0:T(1,128)} %present_h.1, f32[8,8192]{1,0:T(8,128)} %interp_h.1, f32[8,8192]{1,0:T(8,128)} %phase_h.1, f32[316,8,128]{2,1,0:T(8,128)} %bitcast.16, s32[8,16]{1,0:T(8,128)} %bitcast.18, s32[8,16]{1,0:T(8,128)} %bitcast.19, s32[16]{0:T(128)} %list_len_h.1), custom_call_target="tpu_custom_call" | custom-call | tf_op jit(solution)/shard_map/pallas_call | solution.py:291
  10.9 0.7 %copy.13 = f32[2,16,2,1,512]{4,3,2,1,0:T(1,128)} copy(f32[2,16,2,1,512]{4,3,2,1,0:T(1,128)S(1)} %bitcast.15) | data formatting | bytes 262144

commit v10 on v9

--- a/solution.py
+++ b/solution.py
@@ -186,23 +186,15 @@
             [sublane_sums(real, sub), sublane_sums(imag, sub)], axis=0
         ).astype(BF16)
 
-    def post(block, may_be_own):
+    def post(block, own):
         for step in range(grp_size):
-
-            def away():
-                pltpu.make_async_remote_copy(
-                    src_ref=send.at[block], dst_ref=recv.at[me], send_sem=send_sem, recv_sem=recv_sem,
-                    device_id=(grp_at(step), block), device_id_type=MESH,
-                ).start()
-
-            if step or not may_be_own:
-                away()
-            else:
-                pl.when(block != my_ang)(away)
-
-                @pl.when(block == my_ang)
-                def _():
-                    pltpu.make_async_copy(send.at[block], recv.at[me], recv_sem).start()
+            if own and not step:
+                pltpu.make_async_copy(send.at[block], recv.at[me], recv_sem).start()
+                continue
+            pltpu.make_async_remote_copy(
+                src_ref=send.at[block], dst_ref=recv.at[me], send_sem=send_sem, recv_sem=recv_sem,
+                device_id=(grp_at(step), block), device_id_type=MESH,
+            ).start()
 
     def block_at(step):
         return ang_at(1 + step)
@@ -215,22 +207,20 @@
         for i in range(unroll):
             combine(block_at(group * unroll + i), stages.at[i])
 
-    def post_group(group):
-        for i in range(unroll):
-            post(block_at(group * unroll + i), i == unroll - 1)
-
     def one_group(group, carry):
         refine_group(group, stage)
         combine_group(group, stage)
-
-        @pl.when(group == 0)
-        def _():
-            pl.semaphore_wait(barrier, devices - 1)
-
-        post_group(group)
         return carry
 
     lax.fori_loop(0, ang_size // unroll, one_group, 0)
+    pl.semaphore_wait(barrier, devices - 1)
+
+    def post_step(step, carry):
+        post(block_at(step), False)
+        return carry
+
+    lax.fori_loop(0, ang_size - 1, post_step, 0, unroll=5 if ang_size % 5 == 1 else 1)
+    post(my_ang, True)
 
     for load in loads[4:]:
         load.wait()

time: 11.7 us -> 12.1 us (1.034)
  Pallas kernels: 10.9 us -> 11.3 us
    pallas_call x1, Pallas kernels: 10.9 us -> 11.3 us  [local(): pl.pallas_call(functools.partial(kernel, grp_size, ang_size, UNROLL), out...]
where the time goes in v10:
time: 12.1 us; the launch traced here: 12 us
  Pallas kernels  11.3 us (93%)
  local copies, waits for them, and re-layouts  0.66 us (5%)
    pallas_call x1, Pallas kernels, local(): pl.pallas_call(functools.partial(kernel, grp_size, ang_size, UNROLL), out...  11.3 us
    unnamed x1, local copies, waits for them, and re-layouts  0.66 us

profile of v10, /device:TPU:0, one launch (start us, length us, event | category | flops | bytes accessed | tf_op | source)
XLA Modules:
  0.0 12.0 jit_solution(543929921025428175)
XLA Ops:
  0.0 11.3 %shard_map.82 = f32[2,16,8,128]{3,2,1,0:T(8,128)S(1)} custom-call(bf16[32,16,128]{2,1,0:T(8,128)(2,1)} %bitcast.17, s32[1,8]{1,0:T(1,128)} %present_h.1, f32[8,8192]{1,0:T(8,128)} %interp_h.1, f32[8,8192]{1,0:T(8,128)} %phase_h.1, f32[316,8,128]{2,1,0:T(8,128)} %bitcast.16, s32[8,16]{1,0:T(8,128)} %bitcast.18, s32[8,16]{1,0:T(8,128)} %bitcast.19, s32[16]{0:T(128)} %list_len_h.1), custom_call_target="tpu_custom_call" | custom-call | tf_op jit(solution)/shard_map/pallas_call | solution.py:281
  11.3 0.7 %copy.13 = f32[2,16,2,1,512]{4,3,2,1,0:T(1,128)} copy(f32[2,16,2,1,512]{4,3,2,1,0:T(1,128)S(1)} %bitcast.15) | data formatting | bytes 262144

commit v11 on v5

--- a/solution.py
+++ b/solution.py
@@ -75,7 +75,7 @@
         (trans_h, trans), (sources_h, sources), (trans_ids_h, trans_ids), (list_len_h, list_len),
     )
     loads = [pltpu.make_async_copy(src, dst, load_sems.at[i]) for i, (src, dst) in enumerate(pairs)]
-    for load in loads:
+    for load in loads[:4]:
         load.start()
 
     barrier = pltpu.get_barrier_semaphore()
@@ -133,6 +133,8 @@
 
     loads[2].wait()
     loads[3].wait()
+    for load in loads[4:]:
+        load.start()
 
     band_rows = 48
     gap = iota((band_rows, LANES), 0) - iota((band_rows, LANES), 1) // 4
@@ -206,14 +208,17 @@
             post(block_at(group * unroll + i), last and i == unroll - 1)
 
     def one_round(step, last=False):
+        first = isinstance(step, int) and step == 0
         refine_group(2 * step + 1, stage_b)
         combine_group(2 * step, stage_a)
-        if isinstance(step, int) and step == 0:
-            pl.semaphore_wait(barrier, devices - 1)
-        post_group(2 * step)
+        if not first:
+            post_group(2 * step)
         if not last:
             refine_group(2 * step + 2, stage_a)
         combine_group(2 * step + 1, stage_b)
+        if first:
+            pl.semaphore_wait(barrier, devices - 1)
+            post_group(2 * step)
         post_group(2 * step + 1, last)
 
     def advance(step, carry):

time: 11.5 us -> 11.6 us (level)
  the two profiles are of different devices: /device:TPU:1 before, /device:TPU:0 now
where the time goes in v11:
time: 11.6 us; the launch traced here: 11.4 us
  Pallas kernels  10.7 us (92%)
  local copies, waits for them, and re-layouts  0.66 us (6%)
    pallas_call x1, Pallas kernels, local(): pl.pallas_call(functools.partial(kernel, grp_size, ang_size, UNROLL), out...  10.7 us
    unnamed x1, local copies, waits for them, and re-layouts  0.66 us

profile of v11, /device:TPU:0, one launch (start us, length us, event | category | flops | bytes accessed | tf_op | source)
XLA Modules:
  0.0 11.4 jit_solution(16382749808089370848)
XLA Ops:
  0.0 10.7 %shard_map.82 = f32[2,16,8,128]{3,2,1,0:T(8,128)S(1)} custom-call(bf16[32,16,128]{2,1,0:T(8,128)(2,1)} %bitcast.17, s32[1,8]{1,0:T(1,128)} %present_h.1, f32[8,8192]{1,0:T(8,128)} %interp_h.1, f32[8,8192]{1,0:T(8,128)} %phase_h.1, f32[316,8,128]{2,1,0:T(8,128)} %bitcast.16, s32[8,16]{1,0:T(8,128)} %bitcast.18, s32[8,16]{1,0:T(8,128)} %bitcast.19, s32[16]{0:T(128)} %list_len_h.1), custom_call_target="tpu_custom_call" | custom-call | tf_op jit(solution)/shard_map/pallas_call | solution.py:292
  10.8 0.7 %copy.13 = f32[2,16,2,1,512]{4,3,2,1,0:T(1,128)} copy(f32[2,16,2,1,512]{4,3,2,1,0:T(1,128)S(1)} %bitcast.15) | data formatting | bytes 262144
